TPU v7x, 32 devices: a whole 2x2x4 slice. The times are simulated.
32 devices in a mesh: seq: 8 (over z, x), stream: 4 (over y, core).
Axes of the slice: x: 2, y: 2, z: 4, core: 2. Of those that a mesh axis runs over, the one named last changes fastest.
Arguments:
- enc_in: bfloat16 [4, 4, 1024, 512], P(None, 'stream', 'seq'), may hold values from -6 to 6
- dec_in: bfloat16 [4, 4, 1024, 512], P(None, 'stream', 'seq'), may hold values from -6 to 6
- cotangent: bfloat16 [4, 4, 1024, 512], P(None, 'stream', 'seq'), may hold values from -6 to 6
- lengths: int32 [4, 4, 16], P(None, 'stream'), may hold values from 1 to 256, 1024 in all within a row
- attn_master: float32 [6144, 512], P(('seq', 'stream')), may hold values from -0.25 to 0.25
- ffn_in_master: float32 [1024, 2048], P(('seq', 'stream')), may hold values from -0.25 to 0.25
- ffn_out_master: float32 [4096, 512], P(('seq', 'stream')), may hold values from -0.125 to 0.125
- norm_master: float32 [5120], P(('seq', 'stream')), may hold values from -0.5 to 3.9
- attn_first: float32 [6144, 512], P(('seq', 'stream')), may hold values from -256 to 256
- ffn_in_first: float32 [1024, 2048], P(('seq', 'stream')), may hold values from -256 to 256
- ffn_out_first: float32 [4096, 512], P(('seq', 'stream')), may hold values from -256 to 256
- norm_first: float32 [5120], P(('seq', 'stream')), may hold values from -256 to 256
- attn_second: float32 [6144, 512], P(('seq', 'stream')), may hold values from 819.2 to 13107.2
- ffn_in_second: float32 [1024, 2048], P(('seq', 'stream')), may hold values from 819.2 to 13107.2
- ffn_out_second: float32 [4096, 512], P(('seq', 'stream')), may hold values from 819.2 to 13107.2
- norm_second: float32 [5120], P(('seq', 'stream')), may hold values from 819.2 to 13107.2
Outputs:
- enc_out: bfloat16 [4, 4, 1024, 512], P(None, 'stream', 'seq')
- dec_out: bfloat16 [4, 4, 1024, 512], P(None, 'stream', 'seq')
- enc_in_grad: float32 [4, 4, 1024, 512], P(None, 'stream', 'seq')
- dec_in_grad: float32 [4, 4, 1024, 512], P(None, 'stream', 'seq')
- attn_grad: float32 [6144, 512], P(('seq', 'stream'))
- ffn_in_grad: float32 [1024, 2048], P(('seq', 'stream'))
- ffn_out_grad: float32 [4096, 512], P(('seq', 'stream'))
- norm_grad: float32 [5120], P(('seq', 'stream'))
- attn_new: float32 [6144, 512], P(('seq', 'stream'))
- ffn_in_new: float32 [1024, 2048], P(('seq', 'stream'))
- ffn_out_new: float32 [4096, 512], P(('seq', 'stream'))
- norm_new: float32 [5120], P(('seq', 'stream'))
- attn_first_new: float32 [6144, 512], P(('seq', 'stream'))
- ffn_in_first_new: float32 [1024, 2048], P(('seq', 'stream'))
- ffn_out_first_new: float32 [4096, 512], P(('seq', 'stream'))
- norm_first_new: float32 [5120], P(('seq', 'stream'))
- attn_second_new: float32 [6144, 512], P(('seq', 'stream'))
- ffn_in_second_new: float32 [1024, 2048], P(('seq', 'stream'))
- ffn_out_second_new: float32 [4096, 512], P(('seq', 'stream'))
- norm_second_new: float32 [5120], P(('seq', 'stream'))
- attn_copy: bfloat16 [6144, 512], P(('seq', 'stream'))
- ffn_in_copy: bfloat16 [1024, 2048], P(('seq', 'stream'))
- ffn_out_copy: bfloat16 [4096, 512], P(('seq', 'stream'))
- norm_copy: bfloat16 [5120], P(('seq', 'stream'))
- norms: float32 [2, 26], replicated
- trust: float32 [26], replicated
Inputs may be any that keep to these rules, and one draw needn't show every extreme that they name: Each stream's 16 lengths sum to 1024, and the longest of each stream is exactly 256.
All inputs are finite; a program needn't handle non-finite values.
Results may differ from a plain program's by a relative error of at most 0.038.
The roundings to bfloat16 on the way count: a program that leaves them out, or rounds other values in their place, can miss the bound.
Values may be sent and summed in bfloat16 or wider, within the bound.
No kernel may reach another device: no remote copies, remote signals or barrier semaphores. Data moves between devices by JAX's collectives and lax.ppermute only.
A program may use at most 256 MiB of HBM per device.

v0:
```python
import types

import jax
import jax.numpy as jnp
from jax import lax
from jax.experimental import pallas as pl
from jax.experimental.pallas import tpu as pltpu
from jax.sharding import Mesh
from jax.sharding import PartitionSpec as P

HEADS = 8
STEP = 5
HALO = 256
TILE = 256

norm_eps = 1e-05
beta_one = 0.5
beta_two = 0.5
lamb_eps = 1e-06
weight_decay = 0.01
learn_rate = 0.5
masked_score = -1e30

BF = jnp.bfloat16
F32 = jnp.float32
MIB = 1024 * 1024


def dot_nn(a, b):
    return lax.dot_general(a, b, (((1,), (0,)), ((), ())), preferred_element_type=F32)


def dot_nt(a, b):
    return lax.dot_general(a, b, (((1,), (1,)), ((), ())), preferred_element_type=F32)


def dot_tn(a, b):
    return lax.dot_general(a, b, (((0,), (0,)), ((), ())), preferred_element_type=F32)


def norm_parts(rows):
    centre = rows - jnp.mean(rows, axis=-1, keepdims=True)
    inv = lax.rsqrt(jnp.mean(centre * centre, axis=-1, keepdims=True) + norm_eps)
    return centre * inv, inv


def norm_rows(rows, gain, bias):
    return norm_parts(rows)[0] * gain + bias


def norm_back(rows, gain, grad):
    unit, inv = norm_parts(rows)
    lead = grad * gain
    back = inv * (
        lead
        - jnp.mean(lead, axis=-1, keepdims=True)
        - unit * jnp.mean(lead * unit, axis=-1, keepdims=True)
    )
    return (
        back,
        jnp.sum(grad * unit, axis=0, keepdims=True),
        jnp.sum(grad, axis=0, keepdims=True),
    )


gelu_a = 0.7978845608028654
gelu_b = 0.044715


def gelu(v):
    return 0.5 * v * (1.0 + jnp.tanh(gelu_a * (v + gelu_b * (v * v * v))))


def gelu_both(v):
    sq = v * v
    t = jnp.tanh(gelu_a * (v + gelu_b * (sq * v)))
    half = 0.5 * (1.0 + t)
    slope = half + 0.5 * v * (1.0 - t * t) * (gelu_a * (1.0 + 3.0 * gelu_b * sq))
    return v * half, slope


def lane_low(shape):
    return lax.broadcasted_iota(jnp.int32, shape, 1) < 64


def shape_of(dtype, *dims):
    return jax.ShapeDtypeStruct(dims, dtype)


class Fetched:
    def __init__(self, ref, copies):
        self.ref, self.copies, self.shape = ref, copies, ref.shape

    def __getitem__(self, index):
        for copy in self.copies:
            copy.wait()
        self.copies = ()
        return self.ref[index]


def square(array, start, index):
    places, _, width = array.shape
    per = 6 * width // places
    pieces = []
    row, end = index * width, index * width + width
    while row < end:
        place, at = divmod(row, per)
        take = min(per - at, end - row)
        spot = slice(row - index * width, row - index * width + take)
        pieces.append(((place, slice(start + at, start + at + take)), spot))
        row += take
    return (array, (width, width), tuple(pieces))


def rows_of(array, start, count):
    places, _, width = array.shape
    every = slice(0, places)
    return (array, (places, count, width), (((every, slice(start, start + count)), every),))


def fused(name, program, core, small, ins, outs, flops, scratch=(), order=()):
    big, sources = [], []
    for item in ins.values():
        array = item[0] if isinstance(item, tuple) else item
        known = [index for index, other in enumerate(big) if other is array]
        sources.append(known[0] if known else len(big))
        if not known:
            big.append(array)
    shapes = [item[1] if isinstance(item, tuple) else item.shape for item in ins.values()]
    pieces = [item[2] if isinstance(item, tuple) else None for item in ins.values()]
    kinds = [big[source].dtype for source in sources]
    counts = [len(item) if item else 1 for item in pieces]
    n_small, n_big, n_out, extra = len(small), len(big), len(outs), len(order)

    def body(core_ref, *refs):
        small_refs, refs = refs[:n_small], refs[n_small:]
        big_refs, refs = refs[:n_big], refs[n_big + extra :]
        out_refs, refs = refs[:n_out], refs[n_out:]
        in_bufs, refs = refs[: len(ins)], refs[len(ins) :]
        out_bufs, refs = refs[:n_out], refs[n_out:]
        user, (in_sem, out_sem) = refs[:-2], refs[-2:]
        env = types.SimpleNamespace(**dict(zip(small, small_refs)))
        used, fetched = 0, []
        for key, source, piece, buf in zip(ins, sources, pieces, in_bufs):
            src = big_refs[source]
            copies = []
            for item in piece or (None,):
                if item is None:
                    copy = pltpu.make_async_copy(src, buf, in_sem.at[used])
                else:
                    copy = pltpu.make_async_copy(src.at[item[0]], buf.at[item[1]], in_sem.at[used])
                copy.start()
                copies.append(copy)
                used += 1
            setattr(env, key, Fetched(buf, copies))
            fetched.append(getattr(env, key))
        for key, buf in zip(outs, out_bufs):
            setattr(env, key, buf)
        leaving = [None] * n_out

        def store(*bufs):
            for buf in bufs:
                (index,) = [place for place in range(n_out) if out_bufs[place] is buf]
                leaving[index] = pltpu.make_async_copy(buf, out_refs[index], out_sem.at[index])
                leaving[index].start()

        program(env, core_ref, store, *user)
        store(*[buf for buf, copy in zip(out_bufs, leaving) if copy is None])
        for copy in leaving:
            copy.wait()
        for item in fetched:
            for copy in item.copies:
                copy.wait()

    vmem = pl.BlockSpec(memory_space=pltpu.VMEM)
    anywhere = pl.BlockSpec(memory_space=pl.ANY)
    size = sum(array.size * array.dtype.itemsize for array in big)
    results = pl.pallas_call(
        body,
        in_specs=[pl.BlockSpec(memory_space=pltpu.SMEM)] + [vmem] * n_small + [anywhere] * (n_big + extra),
        out_specs=tuple([anywhere] * n_out),
        out_shape=tuple(outs.values()),
        scratch_shapes=[pltpu.VMEM(shape, dtype) for shape, dtype in zip(shapes, kinds)]
        + [pltpu.VMEM(out.shape, out.dtype) for out in outs.values()]
        + list(scratch)
        + [pltpu.SemaphoreType.DMA((sum(counts),)), pltpu.SemaphoreType.DMA((n_out,))],
        compiler_params=pltpu.CompilerParams(vmem_limit_bytes=56 * MIB),
        cost_estimate=pl.CostEstimate(flops=flops, bytes_accessed=size, transcendentals=0),
        name=name,
    )(core, *small.values(), *big, *order)
    return types.SimpleNamespace(**dict(zip(outs, results)))


def tiles_of(core, rows, window):
    if window == rows + HALO:
        near = pl.multiple_of(core[1], HALO)
        return ((near, 0), (pl.multiple_of(rows - TILE - core[1], HALO), None))
    return ((0, 0), (rows - TILE, 1))


def key_rows(ref, lanes, rows, halo):
    if halo is None:
        return ref[0:rows, lanes]
    if halo == 0:
        return ref[0 : rows + HALO, lanes]
    return jnp.concatenate((ref[0:rows, lanes], ref[rows + HALO : rows + 2 * HALO, lanes]), axis=0)


def key_lanes(ref, row, rows, halo):
    if halo is None:
        return ref[row : row + 1, 0:rows]
    if halo == 0:
        return ref[row : row + 1, 0 : rows + HALO]
    return jnp.concatenate(
        (ref[row : row + 1, 0:rows], ref[row : row + 1, rows + HALO : rows + 2 * HALO]), axis=1
    )


def halves(shape):
    low = lane_low(shape)
    return low, ~low


def keep(mask, values):
    return jnp.where(mask, values, jnp.zeros_like(values))


def gain_rows(gains, index):
    return gains[index : index + 1, :], gains[index + 1 : index + 2, :]


def attn_fwd(core, causal, low_src, base, kv_src, weights, qcol, krow, q_out, k_out, v_out, o_out, lse_out, res_out):
    rows, _ = q_out.shape
    window = k_out.shape[0]
    w_q, w_k, w_v, w_o = weights
    queries = dot_nn(low_src(), w_q[...])
    q_out[...] = (queries.astype(BF).astype(F32) * 0.125).astype(BF)
    k_out[...] = dot_nn(kv_src[...], w_k[...]).astype(BF)
    v_out[...] = dot_nn(kv_src[...], w_v[...]).astype(BF)
    for offset, halo in tiles_of(core, rows, window):
        spot = pl.ds(offset, TILE)
        allowed = qcol[spot, 0:1] == key_lanes(krow, 0, rows, halo)
        if causal:
            allowed = allowed & (key_lanes(krow, 1, rows, halo) <= qcol[spot, 1:2])
        lane = lax.broadcasted_iota(jnp.int32, (TILE, 128), 1)
        packed = jnp.zeros((TILE, 128), F32)
        for pair in range(HEADS // 2):
            lanes = slice(pair * 128, pair * 128 + 128)
            q2 = q_out[spot, lanes]
            k2 = key_rows(k_out, lanes, rows, halo)
            v2 = key_rows(v_out, lanes, rows, halo)
            mixed = None
            for half in range(2):
                scores = dot_nt(keep(halves(q2.shape)[half], q2), k2)
                scores = jnp.where(allowed, scores, masked_score)
                top = jnp.max(scores, axis=-1, keepdims=True)
                weights = jnp.exp(scores - top)
                total = jnp.sum(weights, axis=-1, keepdims=True)
                probs = (weights * (1.0 / total)).astype(BF)
                part = dot_nn(probs, keep(halves(v2.shape)[half], v2))
                mixed = part if mixed is None else mixed + part
                packed = jnp.where(lane == 2 * pair + half, top + jnp.log(total), packed)
            o_out[spot, lanes] = mixed.astype(BF)
        lse_out[:, spot] = jnp.transpose(packed)[0:HEADS, :]
    res_out[...] = base() + dot_nn(o_out[...], w_o[...])


def score_grads(q2, do2, k2, v2, allowed, lse, delta):
    sums = None
    for half in range(2):
        qh = keep(halves(q2.shape)[half], q2)
        doh = keep(halves(do2.shape)[half], do2)
        scores = jnp.where(allowed, dot_nt(k2, qh), masked_score)
        probs = jnp.exp(scores - lse[half])
        gscores = (probs * (dot_nt(v2, doh) - delta[half])).astype(BF)
        parts = (
            dot_tn(gscores, keep(halves(k2.shape)[half], k2)),
            dot_nn(gscores, qh),
            dot_nn(probs.astype(BF), doh),
        )
        sums = parts if sums is None else tuple(a + b for a, b in zip(sums, parts))
    return sums


def attn_head(
    core, causal, grad, resid, o_in, q_in, k_in, v_in, lse_in, weights, gains, gain_at, qrow, kcol, e,
):
    back_out, do_out, delta_out, dwo_out, halo_out, dqh_out, ng_out = e.back, e.do, e.delta, e.dwo, e.halo, e.dqh, e.ng
    w_k, w_v, w_o = weights
    rows, width = do_out.shape
    window = k_in.shape[0]
    back, dgain, dbias = norm_back(resid[...], gain_rows(gains, gain_at)[0], grad)
    back_out[...] = back
    ng_out[0:1, :] = dgain
    ng_out[1:2, :] = dbias
    branch = back.astype(BF)
    do_out[...] = dot_nt(branch, w_o[...]).astype(BF)
    mixed = do_out[...].astype(F32) * o_in[...].astype(F32)
    high = mixed.astype(BF)
    rest = (mixed - high.astype(F32)).astype(BF)
    head = lax.broadcasted_iota(jnp.int32, (16, width), 1) // (width // HEADS)
    which = (head == lax.broadcasted_iota(jnp.int32, (16, width), 0)).astype(F32).astype(BF)
    delta_out[...] = (dot_nt(which, high) + dot_nt(which, rest))[0:HEADS, :]
    for offset, halo in tiles_of(core, rows, window):
        if halo is None:
            continue
        spot = pl.ds(offset, TILE)
        keys = slice(rows + halo * HALO, rows + halo * HALO + HALO)
        here = slice(halo * HALO, halo * HALO + HALO)
        allowed = kcol[keys, 0:1] == qrow[0:1, spot]
        if causal:
            allowed = allowed & (kcol[keys, 1:2] <= qrow[1:2, spot])
        for pair in range(HEADS // 2):
            lanes = slice(pair * 128, pair * 128 + 128)
            heads = (2 * pair, 2 * pair + 1)
            dq2, dk2, dv2 = score_grads(
                q_in[spot, lanes],
                do_out[spot, lanes],
                k_in[keys, lanes],
                v_in[keys, lanes],
                allowed,
                [lse_in[h : h + 1, spot] for h in heads],
                [delta_out[h : h + 1, spot] for h in heads],
            )
            dqh_out[here, lanes] = dq2
            halo_out[0, here, lanes] = dk2.astype(BF)
            halo_out[1, here, lanes] = dv2.astype(BF)
    e.gxh[...] = (dot_nt(halo_out[0], w_k[...]) + dot_nt(halo_out[1], w_v[...])).astype(BF)
    dwo_out[...] = dot_tn(o_in[...], branch).astype(BF)


def attn_body(
    core, causal, window, back, do_in, delta, dqh, low_src, q_in, k_in, v_in, lse_in, w_q, qrow, kcol,
    gq_out, dwq_out, own_out, dq_scr,
):
    rows, width = gq_out.shape
    for tile in range(rows // TILE):
        spot = slice(tile * TILE, tile * TILE + TILE)
        allowed = kcol[0:rows, 0:1] == qrow[0:1, spot]
        if causal:
            allowed = allowed & (kcol[0:rows, 1:2] <= qrow[1:2, spot])
        for pair in range(HEADS // 2):
            lanes = slice(pair * 128, pair * 128 + 128)
            heads = (2 * pair, 2 * pair + 1)
            dq2, dk2, dv2 = score_grads(
                q_in[spot, lanes],
                do_in[spot, lanes],
                k_in[0:rows, lanes],
                v_in[0:rows, lanes],
                allowed,
                [lse_in[h : h + 1, spot] for h in heads],
                [delta[h : h + 1, spot] for h in heads],
            )
            dq_scr[spot, lanes] = dq2
            if tile == 0:
                own_out[0, :, lanes] = dk2
                own_out[1, :, lanes] = dv2
            else:
                own_out[0, :, lanes] += dk2
                own_out[1, :, lanes] += dv2
    for offset, halo in tiles_of(core, rows, window):
        if halo is not None:
            dq_scr[pl.ds(offset, TILE), :] += dqh[halo * HALO : halo * HALO + HALO, :]
    grad_q = (dq_scr[...] * 0.125).astype(BF)
    gq_out[...] = back[...] + dot_nt(grad_q, w_q[...])
    dwq_out[...] = dot_tn(low_src(), grad_q).astype(BF)


def split_places(core, source, kept, sent):
    for parity in range(2):

        @pl.when(core[0] == parity)
        def place():
            for chip in range(kept.shape[0]):
                kept[chip] = source[2 * chip + parity]
                sent[chip] = source[2 * chip + 1 - parity]


def kv_bwd(window_rows, own, halo, w_k, w_v):
    rows = own.shape[1]
    window = window_rows.shape[0]
    dk = own[0].astype(BF)
    dv = own[1].astype(BF)
    total = dot_nt(dk, w_k[...]) + dot_nt(dv, w_v[...])
    dwk = dot_tn(window_rows[0:rows, :], dk) + dot_tn(window_rows[rows:window, :], halo[0])
    dwv = dot_tn(window_rows[0:rows, :], dv) + dot_tn(window_rows[rows:window, :], halo[1])
    return total, dwk.astype(BF), dwv.astype(BF)


def lay_out(stack, mats):
    places, _, width = stack.shape
    per = 6 * width // places
    for slot, matrix in enumerate(mats):
        row, end = slot * width, slot * width + width
        while row < end:
            place, start = divmod(row, per)
            take = min(per - start, end - row)
            at = row - slot * width
            stack[place, start : start + take, :] = matrix[at : at + take, :]
            row += take


def up_tile(pack, tile):
    places, _, width = pack.shape
    return pack[:, 128 + 32 * tile : 160 + 32 * tile, :].reshape(places * 32, width)


def down_tile(pack, tile):
    return pack[4 * tile : 4 * tile + 4, 0:128, :].reshape(512, pack.shape[2])


def ffn_fwd(resid, base, gains, gain_in, gain_out, pack, res_out, low_out, hid_low=None, pre=None):
    hidden = norm_rows(resid[...], *gain_rows(gains, gain_in))
    low = hidden.astype(BF)
    if hid_low is not None:
        hid_low[...] = low
    res_out[...] = hidden + base[...].astype(F32)
    for tile in range(4):
        values = dot_nn(low, up_tile(pack, tile))
        if pre is not None:
            pre[tile] = values
        res_out[...] += dot_nn(gelu(values).astype(BF), down_tile(pack, tile))
    low_out[...] = norm_rows(res_out[...], *gain_rows(gains, gain_out)).astype(BF)


def ffn_bwd(grad, res_late, gains, gain_out, pack, gh_out, late_out, ng_out, hid_low, late_low, dpack, pre=None):
    back, dgain, dbias = norm_back(res_late[...], gain_rows(gains, gain_out)[0], grad)
    late_out[...] = back
    gh_out[...] = back
    late_low[...] = back.astype(BF)
    ng_out[0:1, :] = dgain
    ng_out[1:2, :] = dbias
    places, _, width = dpack.shape
    for tile in range(4):
        activ, slope = gelu_both(dot_nn(hid_low[...], up_tile(pack, tile)) if pre is None else pre[tile])
        grad_down = dot_tn(activ.astype(BF), late_low[...]).astype(BF)
        dpack[4 * tile : 4 * tile + 4, 0:128, :] = grad_down.reshape(4, 128, width)
        grad_act = dot_nt(late_low[...], down_tile(pack, tile)).astype(BF).astype(F32)
        grad_pre = (grad_act * slope).astype(BF)
        grad_up = dot_tn(hid_low[...], grad_pre).astype(BF)
        dpack[:, 128 + 32 * tile : 160 + 32 * tile, :] = grad_up.reshape(places, 32, width)
        gh_out[...] += dot_nt(grad_pre, up_tile(pack, tile))


def kept_shapes(rows, window, width, with_o=True):
    outs = dict(
        q=shape_of(BF, rows, width),
        k=shape_of(BF, window, width),
        v=shape_of(BF, window, width),
        lse=shape_of(F32, HEADS, rows),
    )
    return dict(outs, o=shape_of(BF, rows, width)) if with_o else outs


def head_shapes(rows, window, width):
    return dict(
        back=shape_of(F32, rows, width),
        do=shape_of(BF, rows, width),
        delta=shape_of(F32, HEADS, rows),
        dwo=shape_of(BF, width, width),
        halo=shape_of(BF, 2, window - rows, width),
        gxh=shape_of(BF, window - rows, width),
        dqh=shape_of(F32, window - rows, width),
        ng=shape_of(F32, 2, width),
    )


def weights_of(env):
    return env.wq, env.wk, env.wv, env.wo


def named_mats(mats):
    return dict(wq=mats[0], wk=mats[1], wv=mats[2], wo=mats[3])


def enc_forward(x, window_rows, mats, pack, gains, places):
    rows, width = x.shape
    window = window_rows.shape[0]

    def program(e, core, store):
        attn_fwd(
            core, False, lambda: e.x[...], lambda: e.x[...].astype(F32), e.window, weights_of(e),
            e.qcol, e.krow, e.q, e.k, e.v, e.o, e.lse, e.resid,
        )
        store(e.q, e.k, e.v, e.o, e.lse, e.resid)
        ffn_fwd(e.resid, e.x, e.gains, 0, 2, e.pack, e.two, e.low)

    return fused(
        "enc_forward",
        program,
        places.core,
        dict(qcol=places.qcol, krow=places.krow, gains=gains),
        dict(x=x, window=window_rows, **named_mats(mats), pack=pack),
        dict(
            kept_shapes(rows, window, width),
            resid=shape_of(F32, rows, width),
            two=shape_of(F32, rows, width),
            low=shape_of(BF, rows, width),
        ),
        28 * rows * width * width + 8 * rows * window * width,
    )


def self_forward(z, window_rows, mats, places):
    rows, width = z.shape
    window = window_rows.shape[0]

    def program(e, core, store):
        attn_fwd(
            core, True, lambda: e.z[...], lambda: e.z[...].astype(F32), e.window, weights_of(e),
            e.qcol, e.krow, e.q, e.k, e.v, e.o, e.lse, e.resid,
        )

    return fused(
        "self_forward",
        program,
        places.core,
        dict(qcol=places.qcol, krow=places.krow),
        dict(z=z, window=window_rows, **named_mats(mats)),
        dict(kept_shapes(rows, window, width), resid=shape_of(F32, rows, width)),
        12 * rows * width * width + 8 * rows * window * width,
    )


def cross_and_ffn(three, window_rows, mats, pack, z, cot, gains, places):
    rows, width = three.shape
    window = window_rows.shape[0]
    count, block = pack[0].shape[0], pack[1][1]
    f32_rows, low_rows = pltpu.VMEM((rows, width), F32), pltpu.VMEM((rows, width), BF)

    def program(e, core, store, o, four, five, gh, hid_low, late_low, pre, dpack):
        def first():
            return norm_rows(e.three[...], *gain_rows(e.gains, 4))

        attn_fwd(
            core, False, lambda: first().astype(BF), first, e.window, weights_of(e),
            e.qcol, e.krow, e.q, e.k, e.v, o, e.lse, four,
        )
        store(e.q, e.k, e.v, e.lse)
        ffn_fwd(four, e.z, e.gains, 6, 8, e.pack, five, e.low, hid_low, pre)
        store(e.low)
        ffn_bwd(
            e.cot[...].astype(F32), five, e.gains, 8, e.pack, gh, e.five, e.ng8,
            hid_low, late_low, dpack, pre,
        )
        split_places(core, dpack, e.kept, e.sent)
        store(e.sent, e.kept, e.five, e.ng8)
        attn_head(
            core, False, gh[...], four, o, e.q, e.k, e.v, e.lse, (e.wk, e.wv, e.wo), e.gains, 6, e.qrow, e.kcol, e,
        )

    return fused(
        "cross_and_ffn",
        program,
        places.core,
        dict(qcol=places.qcol, krow=places.krow, qrow=places.qrow, kcol=places.kcol, gains=gains),
        dict(three=three, wq=mats[0], window=window_rows, wk=mats[1], wv=mats[2], wo=mats[3], z=z, pack=pack, cot=cot),
        dict(
            **kept_shapes(rows, window, width, False),
            low=shape_of(BF, rows, width),
            kept=shape_of(BF, count // 2, block, width),
            sent=shape_of(BF, count // 2, block, width),
            five=shape_of(F32, rows, width),
            ng8=shape_of(F32, 2, width),
            **head_shapes(rows, window, width),
        ),
        68 * rows * width * width + 8 * rows * window * width,
        scratch=[
            low_rows, f32_rows, f32_rows, f32_rows, low_rows, low_rows,
            pltpu.VMEM((4, rows, width), F32), pltpu.VMEM((count, block, width), BF),
        ],
    )


def own_rows(array, rows):
    spot = (slice(0, rows),)
    return (array, (rows, array.shape[1]), ((spot, spot),))


def cross_body_self_head(c, low_window, three, s, cross_mats, self_mats, gains, places):
    rows, width = three.shape
    window = c.k.shape[0]

    def program(e, core, store, grad, dq, own):
        def first():
            return norm_rows(e.three[...], *gain_rows(e.gains, 4)).astype(BF)

        attn_body(
            core, False, window, e.back_c, e.do_c, e.delta_c, e.dqh_c, first, e.q_c, e.k_c,
            e.v_c, e.lse_c, e.wq_c, e.qrow, e.kcol, grad, e.dwq, own, dq,
        )
        e.gx[...], e.dwk[...], e.dwv[...] = kv_bwd(e.low_window, own, e.halo_c, e.wk_c, e.wv_c)
        store(e.dwq, e.gx, e.dwk, e.dwv)
        attn_head(
            core, True, grad[...], e.three, e.o, e.q, e.k, e.v, e.lse, (e.wk, e.wv, e.wo), e.gains, 4,
            e.qrow, e.kcol, e,
        )

    return fused(
        "cross_body_self_head",
        program,
        places.core,
        dict(qrow=places.qrow, kcol=places.kcol, gains=gains),
        dict(
            q_c=c.q,
            do_c=c.do,
            k_c=own_rows(c.k, rows),
            v_c=own_rows(c.v, rows),
            lse_c=c.lse,
            delta_c=c.delta,
            dqh_c=c.dqh,
            back_c=c.back,
            wq_c=cross_mats[0],
            three=three,
            low_window=low_window,
            halo_c=c.halo,
            wk_c=cross_mats[1],
            wv_c=cross_mats[2],
            wo=self_mats[3],
            o=s.o,
            q=s.q,
            k=s.k,
            v=s.v,
            lse=s.lse,
            wk=self_mats[1],
            wv=self_mats[2],
        ),
        dict(
            gx=shape_of(F32, rows, width),
            dwq=shape_of(BF, width, width),
            dwk=shape_of(BF, width, width),
            dwv=shape_of(BF, width, width),
            **head_shapes(rows, window, width),
        ),
        18 * rows * width * width + 10 * rows * window * width,
        scratch=[pltpu.VMEM((rows, width), F32), pltpu.VMEM((rows, width), F32), pltpu.VMEM((2, rows, width), F32)],
    )


def input_body(name, kept, head, src, window_rows, mats, causal, add, layout, grads, norms, group, places, order):
    rows, width = src.shape
    window = kept.k.shape[0]
    block = 6 * width // group + (16 if norms else 0)

    def program(e, core, store, dq, own, gq, stack, lines):
        others = (e.other0, e.other1, e.other2, e.other3, e.other4)
        attn_body(
            core, causal, window, e.back, e.do, e.delta, e.dqh, lambda: e.src[...], e.q, e.k,
            e.v, e.lse, e.wq, e.qrow, e.kcol, gq, e.dwq, own, dq,
        )
        total, dwk, dwv = kv_bwd(e.window, own, e.halo, e.wk, e.wv)
        e.dwk[...] = dwk
        parts = dict(q=e.dwq, k=dwk, v=dwv)
        lay_out(stack, [others[item] if isinstance(item, int) else parts[item] for item in layout])
        if norms:
            lines[...] = jnp.zeros_like(lines)
            for index, item in enumerate((e.ng0, e.ng1, e.ng2, e.ng3, e.ng4)):
                lines[2 * index : 2 * index + 2, :] = item[...]
            for place in range(group):
                stack[place, block - 16 :, :] = lines[...].astype(BF)
        split_places(core, stack, e.kept, e.sent)
        store(e.sent, e.kept)
        e.grad[...] = gq[...] + total + e.add[...]

    grads = tuple(grads) + (head.dwo,) * (5 - len(grads))
    ng = dict(ng0=norms[0], ng1=norms[1], ng2=norms[2], ng3=norms[3], ng4=norms[4]) if norms else {}
    return fused(
        name,
        program,
        places.core,
        dict(qrow=places.qrow, kcol=places.kcol),
        dict(
            q=kept.q,
            do=head.do,
            k=own_rows(kept.k, rows),
            v=own_rows(kept.v, rows),
            lse=kept.lse,
            delta=head.delta,
            dqh=head.dqh,
            back=head.back,
            wq=mats[0],
            src=src,
            window=window_rows,
            halo=head.halo,
            wk=mats[1],
            wv=mats[2],
            other0=grads[0],
            other1=grads[1],
            other2=grads[2],
            other3=grads[3],
            other4=grads[4],
            add=add,
            **ng,
        ),
        dict(
            sent=shape_of(BF, group // 2, block, width),
            kept=shape_of(BF, group // 2, block, width),
            dwq=shape_of(BF, width, width),
            dwk=shape_of(BF, width, width),
            grad=shape_of(F32, rows, width),
        ),
        14 * rows * width * width + 10 * rows * rows * width,
        scratch=[
            pltpu.VMEM((rows, width), F32), pltpu.VMEM((2, rows, width), F32), pltpu.VMEM((rows, width), F32),
            pltpu.VMEM((group, block, width), BF), pltpu.VMEM((16, width), F32),
        ],
        order=order,
    )


def enc_ffn_head(grad, one, two, kept, pack, mats, gains, places, order):
    rows, width = one.shape
    window = kept.k.shape[0]
    count, block = pack[0].shape[0], pack[1][1]

    def program(e, core, store, gh, hid_low, late_low, dpack):
        hid_low[...] = norm_rows(e.one[...], *gain_rows(e.gains, 0)).astype(BF)
        ffn_bwd(
            e.grad[...], e.two, e.gains, 2, e.pack, gh, e.late, e.ng2, hid_low, late_low, dpack
        )
        split_places(core, dpack, e.kept, e.sent)
        store(e.sent, e.kept, e.late, e.ng2)
        attn_head(
            core, False, gh[...], e.one, e.o, e.q, e.k, e.v, e.lse, (e.wk, e.wv, e.wo), e.gains, 0, e.qrow, e.kcol, e,
        )

    return fused(
        "enc_ffn_head",
        program,
        places.core,
        dict(qrow=places.qrow, kcol=places.kcol, gains=gains),
        dict(
            one=one,
            two=two,
            grad=grad,
            pack=pack,
            wo=mats[3],
            wk=mats[1],
            wv=mats[2],
            o=kept.o,
            q=kept.q,
            k=kept.k,
            v=kept.v,
            lse=kept.lse,
        ),
        dict(
            sent=shape_of(BF, count // 2, block, width),
            kept=shape_of(BF, count // 2, block, width),
            late=shape_of(F32, rows, width),
            ng2=shape_of(F32, 2, width),
            **head_shapes(rows, window, width),
        ),
        44 * rows * width * width + 10 * TILE * TILE * width,
        scratch=[
            pltpu.VMEM((rows, width), F32), pltpu.VMEM((rows, width), BF), pltpu.VMEM((rows, width), BF),
            pltpu.VMEM((count, block, width), BF),
        ],
        order=order,
    )


def segments_at(bounds, places, total_len):
    found = jnp.sum((bounds[None, :] <= places[:, None]).astype(jnp.int32), axis=-1)
    return jnp.where((places >= 0) & (places < total_len), found, -1)


def row_squares(values):
    if values.ndim == 2:
        return jnp.sum(values * values, axis=1)
    return values * values


def owner_groups(rows_local, owner, per_group, count):
    group_ids = (owner * rows_local + jnp.arange(rows_local, dtype=jnp.int32)) // per_group
    return group_ids[:, None] == jnp.arange(count, dtype=jnp.int32)[None, :]


def group_sum(onehot, row_values):
    return jnp.sum(jnp.where(onehot, row_values[:, None], 0.0), axis=0)


def lamb_moments(master, grad_rows, first, second):
    first_new = beta_one * first + (1.0 - beta_one) * grad_rows
    second_new = beta_two * second + (1.0 - beta_two) * grad_rows * grad_rows
    update = (
        first_new
        / (1.0 - beta_one**STEP)
        / (jnp.sqrt(second_new / (1.0 - beta_two**STEP)) + lamb_eps)
        + weight_decay * master
    )
    return (first_new, second_new, update)


GROUP = ("lo", "y", "c")
CHIPS = ("lo", "y")
EVERY = ("hi", "lo", "y", "c")


def swap_hi(array):
    return lax.ppermute(array, "hi", [(0, 1), (1, 0)])


def shift_hi(array, distance):
    count = lax.axis_size("hi")
    route = [(i - distance, i) for i in range(count) if i - distance in range(count)]
    return lax.ppermute(array, "hi", route)


def halo_rows(rows_array):
    rows = rows_array.shape[0]
    if lax.axis_size("hi") == 2:
        return swap_hi(jnp.where(lax.axis_index("hi") == 0, rows_array[rows - HALO :], rows_array[:HALO]))
    left = shift_hi(rows_array[rows - HALO :], 1)
    right = shift_hi(rows_array[:HALO], -1)
    return jnp.concatenate((left, right), axis=0)


def halo_return(grads, total):
    rest = total.shape[0] - HALO
    if lax.axis_size("hi") == 2:
        back = swap_hi(grads)
        last = lax.axis_index("hi") == 0
        return back, total + jnp.where(last, jnp.pad(back, ((rest, 0), (0, 0))), jnp.pad(back, ((0, rest), (0, 0))))
    back = jnp.concatenate((shift_hi(grads[HALO:], 1), shift_hi(grads[:HALO], -1)), axis=0)
    return back, total + jnp.pad(back[:HALO], ((0, rest), (0, 0))) + jnp.pad(back[HALO:], ((rest, 0), (0, 0)))


def pack_up(rows):
    count, units = rows.shape
    return rows.reshape(count, 4, units // 4).swapaxes(0, 1).reshape(4 * count, units // 4)


def unpack_up(packed):
    count, width = packed.shape
    return packed.reshape(4, count // 4, width).swapaxes(0, 1).reshape(count // 4, 4 * width)


def swap_core(array):
    return lax.ppermute(array, "c", [(0, 1), (1, 0)])


def tie(array, other):
    bit = lax.slice(other, (0,) * other.ndim, (1,) * other.ndim).reshape(()) * 0
    return array + bit.astype(array.dtype)


def from_parity(mine, other):
    even = lax.axis_index("c") == 0
    full = jnp.stack((jnp.where(even, mine, other), jnp.where(even, other, mine)), axis=1)
    return full.reshape(-1, *mine.shape[1:])


def gather_plain(attn_shard, up_shard, down_shard, norm_shard):
    width = attn_shard.shape[1]
    group = lax.axis_size(GROUP)
    norm_count = norm_shard.shape[0]
    attn = lax.all_gather(attn_shard, EVERY, axis=0, tiled=True)
    down = lax.all_gather(down_shard, EVERY, axis=0, tiled=True).reshape(2, group, -1, width)
    up = lax.all_gather(up_shard, EVERY, axis=0, tiled=True)
    up = up.reshape(2, group, -1, 4, width).swapaxes(2, 3).reshape(2, group, -1, width)
    norms = jnp.pad(norm_shard[None, :], ((0, 0), (0, width - norm_count)))
    norms = lax.all_gather(norms, EVERY, axis=0, tiled=True)[:, :norm_count]
    ffn = jnp.concatenate((down, up), axis=2)
    attn = attn.reshape(2, group, -1, width)
    full = jnp.concatenate((attn[0], attn[1], ffn[0]), axis=1)
    return full, ffn[1], norms.reshape(10, width).astype(F32)


def reduce_cores(kept, sent):
    return (kept.astype(F32) + swap_core(sent).astype(F32)).astype(BF)


def reduce_chips(pair):
    parts = lax.all_to_all(pair, CHIPS, split_axis=0, concat_axis=0, tiled=True)
    return jnp.sum(parts.astype(F32), axis=0)


def join_halves(zero, one):
    first = lax.axis_index("hi") == 0
    mine = jnp.where(first, zero, one)
    sent = jnp.where(first, one, zero).astype(BF)
    return mine + swap_hi(sent).astype(F32)


def reduce_plain(attn0, attn1, ffn0, ffn1, norm_local):
    group, _, width = ffn0.shape

    def scatter(rows):
        return lax.psum_scatter(rows, EVERY, scatter_dimension=0, tiled=True).astype(F32)

    attn = jnp.concatenate((attn0, attn1), axis=0).reshape(-1, width)
    ffn = jnp.stack((ffn0, ffn1)).reshape(2 * group, -1, width)
    up = ffn[:, 128:].reshape(2 * group, 4, 32, width).swapaxes(1, 2).reshape(-1, 4 * width)
    norms = lax.psum_scatter(
        norm_local.reshape(lax.axis_size(EVERY), -1), EVERY, scatter_dimension=0, tiled=True
    )
    return scatter(attn), scatter(up), scatter(ffn[:, :128].reshape(-1, width)), norms[0]


def shards(
    enc_in,
    dec_in,
    cotangent,
    lengths,
    attn_master,
    ffn_in_master,
    ffn_out_master,
    norm_master,
    attn_first,
    ffn_in_first,
    ffn_out_first,
    norm_first,
    attn_second,
    ffn_in_second,
    ffn_out_second,
    norm_second,
):
    micro, _, length_dev, width = enc_in.shape
    rows = micro * length_dev
    hidden_units = ffn_in_master.shape[1]
    high, low = lax.axis_index("hi"), lax.axis_index("lo")
    n_high = lax.axis_size("hi")
    owner = lax.axis_index(EVERY)
    masters = (attn_master, ffn_in_master, ffn_out_master, norm_master)
    group_info = ((width, 12), (width, 2), (hidden_units, 2), (width, 10))
    onehots = [
        owner_groups(master.shape[0], owner, info[0], info[1])
        for master, info in zip(masters, group_info)
    ]
    weight_local = jnp.concatenate(
        [group_sum(onehot, row_squares(master)) for onehot, master in zip(onehots, masters)]
    )

    plain = n_high != 2

    def regroup(*arrays):
        packed = jnp.stack([array[:, 0] for array in arrays], axis=1)
        packed = lax.all_to_all(packed, "lo", split_axis=0, concat_axis=0, tiled=True)
        packed = packed.swapaxes(0, 1).reshape(len(arrays), rows, width)
        return packed

    core = jnp.stack((lax.axis_index("c"), jnp.where(high == 0, rows - HALO, 0))).astype(jnp.int32)
    attn_rows = attn_master.shape[0]
    norm_count = norm_master.shape[0]
    attn_low, up_low, down_low, norm_low = [master.astype(BF) for master in masters]
    if plain:
        full, late, gains = gather_plain(attn_low, up_low, down_low, norm_low)
        enc_rows, dec_rows, cot_rows = regroup(enc_in, dec_in, cotangent)
    else:
        first = high == 0
        norm_pad = jnp.pad(norm_low[None, :], ((0, 15), (0, width - norm_count)))
        mine = jnp.concatenate((attn_low, down_low, pack_up(up_low), norm_pad), axis=0)
        other = swap_hi(mine)
        enc_rows, dec_rows, cot_rows = regroup(enc_in, dec_in, cotangent)
        zero = jnp.where(first, mine, other)
        one = jnp.where(first, other, mine)
        last = mine.shape[0] - 16
        early = (one[:attn_rows], zero[attn_rows : last + 1], one[last:-1])
        early = jnp.concatenate((tie(zero[:attn_rows], enc_rows), *early), axis=0)
        full = lax.all_gather(early, GROUP, axis=0, tiled=False)
        late = lax.all_gather(one[attn_rows:last], GROUP, axis=0, tiled=False)
        gains = full[:, attn_rows + last : attn_rows + last + 2, :norm_count].swapaxes(0, 1)
        gains = gains.reshape(10, width).astype(F32)
    enc_window = jnp.concatenate((enc_rows, halo_rows(enc_rows)), axis=0)
    dec_window = jnp.concatenate((dec_rows, halo_rows(dec_rows)), axis=0)
    group = full.shape[0]

    total_len = rows * n_high
    bounds = jnp.cumsum(lengths[:, 0, :], axis=-1)
    bounds = lax.dynamic_index_in_dim(bounds, low, 0, keepdims=False)
    base = high * rows
    own_pos = base + jnp.arange(rows, dtype=jnp.int32)
    step = jnp.arange(HALO, dtype=jnp.int32)
    if n_high == 2:
        halo_pos = jnp.where(high == 0, rows, rows - HALO) + step
    else:
        halo_pos = jnp.concatenate((base - HALO + step, base + rows + step))
    key_pos = jnp.concatenate((own_pos, halo_pos))
    key_seg = segments_at(bounds, key_pos, total_len)
    krow = jnp.stack((key_seg, key_pos), axis=0)
    kcol = jnp.stack((key_seg, key_pos), axis=1)
    places = types.SimpleNamespace(
        krow=krow,
        kcol=kcol,
        qrow=krow[:, :rows],
        qcol=kcol[:rows],
        core=core,
    )

    per = 6 * width // group
    mats = [square(full, 0, index) for index in range(6)] + [square(full, per, index) for index in range(6)]
    pack0, pack1 = rows_of(full, 2 * per, late.shape[1]), rows_of(late, 0, late.shape[1])
    e = enc_forward(enc_rows, enc_window, mats[0:4], pack0, gains, places)
    low_window = jnp.concatenate((e.low, halo_rows(e.low)), axis=0)
    s = self_forward(dec_rows, dec_window, mats[4:8], places)
    c = cross_and_ffn(s.resid, low_window, mats[8:12], pack1, dec_rows, cot_rows, gains, places)

    def restore(*arrays):
        outs = jnp.stack(arrays, axis=0).reshape(len(arrays), micro, length_dev, width).swapaxes(0, 1)
        return lax.all_to_all(outs, "lo", split_axis=0, concat_axis=0, tiled=True)

    sh = cross_body_self_head(c, low_window, s.resid, s, mats[8:12], mats[4:8], gains, places)
    back_c, grad_encoded = halo_return(c.gxh, sh.gx)
    lows = restore(e.low, c.low)
    pair_f1 = c.kept if plain else reduce_cores(tie(tie(tie(c.kept, sh.ng), lows), back_c), c.sent)
    sb = input_body(
        "self_body", s, sh, dec_rows, dec_window, mats[4:8], True, c.five, ("v", 0, 1, 2, 3, 4),
        (sh.dwo, sh.dwq, sh.dwk, sh.dwv, c.dwo), (), group, places, (pair_f1, back_c),
    )
    back_s, dec_grad = halo_return(sh.gxh, sb.grad)
    if plain:
        pair_a1 = sb.kept
    else:
        part_f1 = reduce_chips(pair_f1)
        pair_a1 = reduce_cores(tie(tie(sb.kept, part_f1), back_s), sb.sent)
    eh = enc_ffn_head(grad_encoded, e.resid, e.two, e, pack0, mats[0:4], gains, places, (pair_a1,))
    if plain:
        pair_f0 = eh.kept
    else:
        part_a1 = reduce_chips(pair_a1)
        pair_f0 = reduce_cores(tie(eh.kept, part_a1), eh.sent)
    eb = input_body(
        "enc_body", e, eh, enc_rows, enc_window, mats[0:4], False, eh.late, ("q", "k", "v", 0, 1, 2),
        (eh.dwo, sb.dwq, sb.dwk), (eh.ng, eh.ng2, sh.ng, c.ng, c.ng8), group, places, (pair_f0,),
    )
    _, enc_grad = halo_return(eh.gxh, eb.grad)
    enc_grad, dec_grad = enc_grad.astype(BF), dec_grad.astype(BF)
    if plain:
        attn_own, up_own, down_own, norm_own = reduce_plain(
            from_parity(eb.kept, eb.sent)[:, :per],
            from_parity(sb.kept, sb.sent),
            from_parity(eh.kept, eh.sent),
            from_parity(c.kept, c.sent),
            jnp.concatenate((eh.ng, eh.ng2, sh.ng, c.ng, c.ng8), axis=0).reshape(n_high, group, norm_count),
        )
        grads = restore(enc_grad, dec_grad)
    else:
        part_f0 = reduce_chips(pair_f0)
        part_a0 = reduce_chips(reduce_cores(eb.kept, eb.sent))
        grads = restore(tie(enc_grad, part_a0), dec_grad)
        ffn_own = join_halves(part_f0, part_f1)
        both = join_halves(part_a0, jnp.concatenate((part_a1, part_a0[attn_rows:]), axis=0))
        attn_own, up_own, down_own = both[:attn_rows], unpack_up(ffn_own[128:]), ffn_own[:128]
        norm_own = lax.dynamic_slice_in_dim(both[attn_rows:].reshape(-1), owner * norm_count, norm_count)

    owned = (attn_own, up_own, down_own, norm_own)
    firsts = (attn_first, ffn_in_first, ffn_out_first, norm_first)
    seconds = (attn_second, ffn_in_second, ffn_out_second, norm_second)
    moments = [
        lamb_moments(masters[index], owned[index], firsts[index], seconds[index])
        for index in range(4)
    ]
    update_local = jnp.concatenate(
        [group_sum(onehots[index], row_squares(moments[index][2])) for index in range(4)]
    )
    squares = jnp.stack((weight_local, update_local))
    squares = jnp.pad(squares, ((0, 6), (0, 128 - squares.shape[1])))
    count = lax.axis_size(EVERY)
    squares = tie(squares, grads)
    squares = jnp.broadcast_to(squares[None], (count,) + squares.shape)
    squares = jnp.sum(lax.all_to_all(squares, EVERY, split_axis=0, concat_axis=0, tiled=True), axis=0)
    norms = jnp.sqrt(squares[:2, :26])
    ratio = norms[0] / norms[1]
    bounds_at = (0, 12, 14, 16, 26)
    new_weights = []
    for index in range(4):
        row_ratio = jnp.sum(
            jnp.where(onehots[index], ratio[None, bounds_at[index] : bounds_at[index + 1]], 0.0), axis=1
        )
        if masters[index].ndim == 2:
            row_ratio = row_ratio[:, None]
        new_weights.append(masters[index] - learn_rate * row_ratio * moments[index][2])
    return (
        lows[:, 0][:, None],
        lows[:, 1][:, None],
        grads[:, 0][:, None].astype(F32),
        grads[:, 1][:, None].astype(F32),
        *owned,
        *new_weights,
        *[item[0] for item in moments],
        *[item[1] for item in moments],
        *[item.astype(BF) for item in new_weights],
        norms,
        ratio,
    )


def solution(mesh):
    count_seq, count_stream = mesh.shape["seq"], mesh.shape["stream"]

    def run(*args):
        micro = args[0].shape[0]
        split = Mesh(
            mesh.devices.reshape(count_seq // micro, micro, count_stream // 2, 2), ("hi", "lo", "y", "c")
        )
        tokens = P(None, ("y", "c"), ("hi", "lo"), None)
        wide = P(EVERY, None)
        flat = P(EVERY)
        owned = (wide, wide, wide, flat)
        return jax.shard_map(
            shards,
            mesh=split,
            in_specs=(tokens, tokens, tokens, P(None, ("y", "c"), None), *owned, *owned, *owned),
            out_specs=(tokens, tokens, tokens, tokens, *owned, *owned, *owned, *owned, *owned, P(), P()),
            check_vma=False,
        )(*args)

    return run
```

profile of v0, /device:TPU:0, one launch (start us, length us, event | category | flops | bytes accessed | tf_op | source)
XLA Modules:
  0.0 441.1 jit_solution(17088233739541396786)
XLA Ops:
  7.2 2.7 pad_maximum_fusion
  9.9 5.4 %all-to-all-start = ((bf16[4,3,128,512]{3,2,1,0:T(8,128)(2,1)}), bf16[4,3,128,512]{3,2,1,0:T(8,128)(2,1)S(1)}, u32[]{:S(2)}, u32[]{:S(2)}) async-start(bf16[4,3,128,512]{3,2,1,0:T(8,128)(2,1)} %pad_maximum_fusion), calls=%async_computation | async-start | bytes 3145728 | tf_op jit(solution)/shard_map/all_to_all | solution.py:938
  15.6 2.7 collective-permute-start
  18.2 24.3 %collective-permute-done = bf16[464,512]{1,0:T(8,128)(2,1)} collective-permute-done((bf16[464,512]{1,0:T(8,128)(2,1)S(1)}, bf16[464,512]{1,0:T(8,128)(2,1)}, u32[]{:S(2)}, u32[]{:S(2)}) %collective-permute-start) | collective-permute-done | bytes 475168 | tf_op jit(solution)/shard_map/ppermute | solution.py:800
  42.5 1.2 broadcast_select_fusion.1
  50.5 3.6 collective-permute-start.1
  56.8 13.6 %collective-permute-done.1 = bf16[256,512]{1,0:T(8,128)(2,1)S(1)} collective-permute-done((bf16[256,512]{1,0:T(8,128)(2,1)S(1)}, bf16[256,512]{1,0:T(8,128)(2,1)S(1)}, u32[]{:S(2)}, u32[]{:S(2)}) %collective-permute-start.1) | collective-permute-done | bytes 262176 | tf_op jit(solution)/shard_map/ppermute | solution.py:800
  71.3 4.8 %collective-permute-done.2 = bf16[256,512]{1,0:T(8,128)(2,1)S(1)} collective-permute-done((bf16[256,512]{1,0:T(8,128)(2,1)S(1)}, bf16[256,512]{1,0:T(8,128)(2,1)S(1)}, u32[]{:S(2)}, u32[]{:S(2)}) %collective-permute-start.2) | collective-permute-done | bytes 262176 | tf_op jit(solution)/shard_map/ppermute | solution.py:800
  77.1 43.4 %all-gather.5.cloned.1.call-done = bf16[10496,512]{1,0:T(8,128)(2,1)} async-done(((bf16[656,512]{1,0:T(8,128)(2,1)}), bf16[10496,512]{1,0:T(8,128)(2,1)}) %all-gather.5.cloned.1.call-update) | async-done | bytes 10747920 | tf_op jit(solution)/shard_map/all_gather | solution.py:960
  122.0 15.3 %enc_forward.1 = (bf16[512,512]{1,0:T(8,128)(2,1)}, bf16[768,512]{1,0:T(8,128)(2,1)}, bf16[768,512]{1,0:T(8,128)(2,1)}, f32[8,512]{1,0:T(8,128)}, bf16[512,512]{...) custom-call(s32[2]{0:T(128)} %pad_add_fusion.3.core_ref, ...), custom_call_target="tpu_custom_call" | custom-call | flops 5368709120 | bytes 12058624 | tf_op jit(solution)/shard_map/enc_forward/pallas_call | solution.py:178
  138.4 2.2 collective-permute-start.3
  141.7 12.9 %self_forward.1 = (bf16[512,512]{1,0:T(8,128)(2,1)}, bf16[768,512]{1,0:T(8,128)(2,1)}, bf16[768,512]{1,0:T(8,128)(2,1)}, f32[8,512]{1,0:T(8,128)}, bf16[512,512]{1,0:T(8,128)(2,1)}, /*index=5*/f32[512,512]{1,0:T(8,128)}) custom-call(s32[2]{0:T(128)} %pad_add_fusion.3.core_ref, s32[512,2]{1,0:T(8,128)} %slice.183.refs_0_, s32[2,768]{1,0:T(2,128)} %pad_add_fusion.refs_1_, ...), custom_call_target="tpu_custom_call" | custom-call | flops 3221225472 | bytes 12058624 | tf_op jit(solution)/shard_map/self_forward/pallas_call | solution.py:178
  154.7 9.4 %all-gather.7.cloned.1.call-done = bf16[4096,512]{1,0:T(8,128)(2,1)} async-done(((bf16[256,512]{1,0:T(8,128)(2,1)}), bf16[4096,512]{1,0:T(8,128)(2,1)}) %all-gather.7.cloned.1.call-update) | async-done | bytes 4194320 | tf_op jit(solution)/shard_map/all_gather | solution.py:961
  164.0 37.9 %cross_and_ffn.1 = (bf16[512,512]{1,0:T(8,128)(2,1)}, bf16[768,512]{1,0:T(8,128)(2,1)}, bf16[768,512]{1,0:T(8,128)(2,1)}, f32[8,512]{1,0:T(8,128)}, bf16[512,512...) custom-call(s32[2]{0:T(128)} %pad_add_fusion.3.core_ref, ...), custom_call_target="tpu_custom_call" | custom-call | flops 10737418240 | bytes 17825792 | tf_op jit(solution)/shard_map/cross_and_ffn/pallas_call | solution.py:178
  202.2 2.2 maximum_bitcast_fusion
  204.4 3.9 all-to-all-start.1
  208.3 2.3 collective-permute-start.4
  210.6 19.5 %cross_body_self_head.1 = (f32[512,512]{1,0:T(8,128)}, bf16[512,512]{1,0:T(8,128)(2,1)}, bf16[512,512]{1,0:T(8,128)(2,1)}, bf16[512,512]{1,0:T(8,128)(2,1)}, f32...) custom-call(s32[2]{0:T(128)} %pad_add_fusion.3.core_ref, ...), custom_call_target="tpu_custom_call" | custom-call | flops 4429185024 | bytes 19972096 | tf_op jit(solution)/shard_map/cross_body_self_head/pallas_call | solution.py:178
  230.1 1.2 slice.157
  234.5 4.4 %add_convert_fusion.1.refs_20_ = bf16[8,256,512]{2,1,0:T(8,128)(2,1)} fusion(bf16[8,256,512]{2,1,0:T(8,128)(2,1)} %collective-permute-done.5, bf16[8,256,512]{2,1,0:T(8,128)(2,1)} %get-tuple-element.126, bf16[]{:T(256)} %bitcast.27, bf16[]{:T(256)} %bitcast.26, bf16[]{:T(256)} %bitcast.25), kind=kLoop, calls=%fused_computation.3 | loop fusion | flops 7340032 | bytes 6291462 | tf_op jit(solution)/shard_map/convert_element_type | solution.py:870
  238.9 5.0 %all-to-all-start.2 = ((bf16[8,256,512]{2,1,0:T(8,128)(2,1)}), bf16[8,256,512]{2,1,0:T(8,128)(2,1)S(1)}, u32[]{:S(2)}, u32[]{:S(2)}) async-start(bf16[8,256,512]{2,1,0:T(8,128)(2,1)} %add_convert_fusion.1.refs_20_), calls=%async_computation.2 | async-start | bytes 4194304 | tf_op jit(solution)/shard_map/all_to_all | solution.py:874
  243.9 15.9 %self_body.1 = (bf16[8,192,512]{2,1,0:T(8,128)(2,1)}, bf16[8,192,512]{2,1,0:T(8,128)(2,1)}, bf16[512,512]{1,0:T(8,128)(2,1)}, bf16[512,512]{1,0:T(8,128)(2,1)}, f32[512,512]{1,0:T(8,128)}) custom-call(s32[2]{0:T(128)} %pad_add_fusion.3.core_ref, s32[2,512]{1,0:T(2,128)} %fusion.6.refs_2_.refs_0_, s32[768,2]{1,0:T(8,128)} %copy-done, ...), custom_call_target="tpu_custom_call" | custom-call | flops 3221225472 | bytes 20480000 | tf_op jit(solution)/shard_map/self_body/pallas_call | solution.py:178
  259.9 1.1 collective-permute-start.6
  261.0 12.0 %collective-permute-done.6 = bf16[256,512]{1,0:T(8,128)(2,1)S(1)} collective-permute-done((bf16[256,512]{1,0:T(8,128)(2,1)S(1)}, bf16[256,512]{1,0:T(8,128)(2,1)S(1)}, u32[]{:S(2)}, u32[]{:S(2)}) %collective-permute-start.6) | collective-permute-done | bytes 262176 | tf_op jit(solution)/shard_map/ppermute | solution.py:800
  276.4 3.2 add_convert_fusion.3.refs_12_
  279.6 6.4 %all-to-all-start.3 = ((bf16[8,192,512]{2,1,0:T(8,128)(2,1)}), bf16[8,192,512]{2,1,0:T(8,128)(2,1)S(1)}, u32[]{:S(2)}, u32[]{:S(2)}) async-start(bf16[8,192,512]{2,1,0:T(8,128)(2,1)} %add_convert_fusion.3.refs_12_), calls=%async_computation.3 | async-start | bytes 3145728 | tf_op jit(solution)/shard_map/all_to_all | solution.py:874
  286.0 2.3 convert_add_fusion.refs_5_
  288.3 18.2 %enc_ffn_head.1 = (bf16[8,256,512]{2,1,0:T(8,128)(2,1)}, bf16[8,256,512]{2,1,0:T(8,128)(2,1)}, f32[512,512]{1,0:T(8,128)}, f32[2,512]{1,0:T(2,128)}, f32[512,512...) custom-call(s32[2]{0:T(128)} %pad_add_fusion.3.core_ref, ...), custom_call_target="tpu_custom_call" | custom-call | flops 6241124352 | bytes 16531456 | tf_op jit(solution)/shard_map/enc_ffn_head/pallas_call | solution.py:178
  308.1 3.1 collective-permute-done.8
  311.1 4.3 add_convert_fusion.refs_23_
  315.4 5.3 %all-to-all-start.6 = ((bf16[8,256,512]{2,1,0:T(8,128)(2,1)}), bf16[8,256,512]{2,1,0:T(8,128)(2,1)S(1)}, u32[]{:S(2)}, u32[]{:S(2)}) async-start(bf16[8,256,512]{2,1,0:T(8,128)(2,1)} %add_convert_fusion.refs_23_), calls=%async_computation.6 | async-start | bytes 4194304 | tf_op jit(solution)/shard_map/all_to_all | solution.py:874
  320.8 16.0 %enc_body.1 = (bf16[8,208,512]{2,1,0:T(8,128)(2,1)}, bf16[8,208,512]{2,1,0:T(8,128)(2,1)}, bf16[512,512]{1,0:T(8,128)(2,1)}, bf16[512,512]{1,0:T(8,128)(2,1)}, f32[512,512]{1,0:T(8,128)}) custom-call(s32[2]{0:T(128)} %pad_add_fusion.3.core_ref, s32[2,512]{1,0:T(2,128)} %fusion.6.refs_2_.refs_0_, s32[768,2]{1,0:T(8,128)} %copy-done, ...), custom_call_target="tpu_custom_call" | custom-call | flops 3221225472 | bytes 19451904 | tf_op jit(solution)/shard_map/enc_body/pallas_call | solution.py:178
  336.8 3.8 collective-permute-done.10
  340.6 3.2 add_convert_fusion.2
  343.8 4.5 %all-to-all-done.6 = bf16[8,256,512]{2,1,0:T(8,128)(2,1)S(1)} async-done(((bf16[8,256,512]{2,1,0:T(8,128)(2,1)}), bf16[8,256,512]{2,1,0:T(8,128)(2,1)S(1)}, u32[]{:S(2)}, u32[]{:S(2)}) %all-to-all-start.6) | async-done | bytes 2097184 | tf_op jit(solution)/shard_map/all_to_all | solution.py:874
  348.3 4.5 %all-to-all-start.4 = ((bf16[8,208,512]{2,1,0:T(8,128)(2,1)}), bf16[8,208,512]{2,1,0:T(8,128)(2,1)}, u32[]{:S(2)}, u32[]{:S(2)}) async-start(bf16[8,208,512]{2,1,0:T(8,128)(2,1)} %add_convert_fusion.2), calls=%async_computation.4 | async-start | bytes 3407872 | tf_op jit(solution)/shard_map/all_to_all | solution.py:874
  352.9 2.2 fusion.19
  355.6 2.0 collective-permute-start.12
  358.8 20.4 %collective-permute-done.12 = bf16[256,512]{1,0:T(8,128)(2,1)S(1)} collective-permute-done((bf16[256,512]{1,0:T(8,128)(2,1)S(1)}, bf16[256,512]{1,0:T(8,128)(2,1)S(1)}, u32[]{:S(2)}, u32[]{:S(2)}) %collective-permute-start.12) | collective-permute-done | bytes 262176 | tf_op jit(solution)/shard_map/ppermute | solution.py:800
  381.7 4.6 %all-to-all-done.4 = bf16[8,208,512]{2,1,0:T(8,128)(2,1)} async-done(((bf16[8,208,512]{2,1,0:T(8,128)(2,1)}), bf16[8,208,512]{2,1,0:T(8,128)(2,1)}, u32[]{:S(2)}, u32[]{:S(2)}) %all-to-all-start.4) | async-done | bytes 1703968 | tf_op jit(solution)/shard_map/all_to_all | solution.py:874
  386.3 1.7 convert_reduce_fusion.2
  389.2 1.5 fusion.1
  391.8 3.5 all-to-all-start.5
  395.9 15.4 %collective-permute-done.11 = bf16[208,512]{1,0:T(8,128)(2,1)S(1)} collective-permute-done((bf16[208,512]{1,0:T(8,128)(2,1)S(1)}, bf16[208,512]{1,0:T(8,128)(2,1)S(1)}, u32[]{:S(2)}, u32[]{:S(2)}) %collective-permute-start.11) | collective-permute-done | bytes 213024 | tf_op jit(solution)/shard_map/ppermute | solution.py:800
  415.4 4.9 %all-to-all-start.7 = ((f32[32,8,128]{2,1,0:T(8,128)}), f32[32,8,128]{2,1,0:T(8,128)S(1)}, u32[]{:S(2)}, u32[]{:S(2)}) async-start(f32[32,8,128]{2,1,0:T(8,128)} %broadcast_in_dim.170), calls=%async_computation.7 | async-start | bytes 262144 | tf_op jit(solution)/shard_map/all_to_all | solution.py:1061
  420.3 1.6 slice_convert_fusion
  421.9 6.6 %all-to-all-done.7 = f32[32,8,128]{2,1,0:T(8,128)S(1)} async-done(((f32[32,8,128]{2,1,0:T(8,128)}), f32[32,8,128]{2,1,0:T(8,128)S(1)}, u32[]{:S(2)}, u32[]{:S(2)}) %all-to-all-start.7) | async-done | bytes 131104 | tf_op jit(solution)/shard_map/all_to_all | solution.py:1061
  431.1 1.9 fusion.11
  (192 shorter events, 32.0 us)
Async XLA Ops:
  9.9 35.3 %all-to-all-start = ((bf16[4,3,128,512]{3,2,1,0:T(8,128)(2,1)}), bf16[4,3,128,512]{3,2,1,0:T(8,128)(2,1)S(1)}, u32[]{:S(2)}, u32[]{:S(2)}) async-start(bf16[4,3,128,512]{3,2,1,0:T(8,128)(2,1)} %pad_maximum_fusion), calls=%async_computation | async-start | bytes 3145728 | tf_op jit(solution)/shard_map/all_to_all | solution.py:938
  15.3 105.2 %all-gather.5.cloned.1.call-start = ((), (), s32[]{:S(2)}) async-start(), calls=%async_computation.8 | async-start | bytes 11419648 | tf_op jit(solution)/shard_map/all_gather | solution.py:960
  15.6 26.9 %collective-permute-start = (bf16[464,512]{1,0:T(8,128)(2,1)S(1)}, bf16[464,512]{1,0:T(8,128)(2,1)}, u32[]{:S(2)}, u32[]{:S(2)}) collective-permute-start(bf16[464,512]{1,0:T(8,128)(2,1)S(1)} %fusion.2), channel_id=1, source_target_pairs={{0,16},{16,0},{1,17},{17,1},{2,18},{18,2},{3,19},{19,3},{4,20},{20... | collective-permute-start | bytes 1425416 | tf_op jit(solution)/shard_map/ppermute | solution.py:800
  46.1 24.3 %copy-start.2 = (bf16[1,4,128,512]{3,2,0,1:T(8,128)(2,1)}, bf16[1,4,128,512]{3,2,0,1:T(8,128)(2,1)S(1)}, u32[]{:S(2)}) copy-start(bf16[1,4,128,512]{3,2,0,1:T(8,128)(2,1)S(1)} %get-tuple-element.189) | copy-start | bytes 1572868
  46.1 30.0 %copy-start.1 = (bf16[1,4,128,512]{3,2,0,1:T(8,128)(2,1)}, bf16[1,4,128,512]{3,2,0,1:T(8,128)(2,1)S(1)}, u32[]{:S(2)}) copy-start(bf16[1,4,128,512]{3,2,0,1:T(8,128)(2,1)S(1)} %get-tuple-element.188) | copy-start | bytes 1572868
  49.2 114.8 %all-gather.7.cloned.1.call-start = ((), (), s32[]{:S(2)}) async-start(), calls=%async_computation.9 | async-start | bytes 4456448 | tf_op jit(solution)/shard_map/all_gather | solution.py:961
  50.5 19.9 %collective-permute-start.1 = (bf16[256,512]{1,0:T(8,128)(2,1)S(1)}, bf16[256,512]{1,0:T(8,128)(2,1)S(1)}, u32[]{:S(2)}, u32[]{:S(2)}) collective-permute-start(bf16[256,512]{1,0:T(8,128)(2,1)S(1)} %bitcast.99), channel_id=1, source_target_pairs={{0,16},{16,0},{1,17},{17,1},{2,18},{18,2},{3,19},{19,3},{4,20},{20... | collective-permute-start | bytes 786440 | tf_op jit(solution)/shard_map/ppermute | solution.py:800
  54.6 21.5 %collective-permute-start.2 = (bf16[256,512]{1,0:T(8,128)(2,1)S(1)}, bf16[256,512]{1,0:T(8,128)(2,1)S(1)}, u32[]{:S(2)}, u32[]{:S(2)}) collective-permute-start(bf16[256,512]{1,0:T(8,128)(2,1)S(1)} %bitcast.98), channel_id=1, source_target_pairs={{0,16},{16,0},{1,17},{17,1},{2,18},{18,2},{3,19},{19,3},{4,20},{20... | collective-permute-start | bytes 786440 | tf_op jit(solution)/shard_map/ppermute | solution.py:800
  55.4 81.9 %copy-start = (s32[768,2]{1,0:T(8,128)}, s32[768,2]{1,0:T(8,128)S(1)}, u32[]{:S(2)}) copy-start(s32[768,2]{1,0:T(8,128)S(1)} %copy.72.refs_3_.refs_1_) | copy-start | bytes 18436
  138.4 16.2 %collective-permute-start.3 = (bf16[256,512]{1,0:T(8,128)(2,1)S(1)}, bf16[256,512]{1,0:T(8,128)(2,1)S(1)}, u32[]{:S(2)}, u32[]{:S(2)}) collective-permute-start(bf16[256,512]{1,0:T(8,128)(2,1)S(1)} %slice_select_fusion.2), channel_id=1, source_target_pairs={{0,16},{16,0},{1,17},{17,1},{2,18},{18,2},{3,19},{19,3},{4,20},{20... | collective-permute-start | bytes 786440 | tf_op jit(solution)/shard_map/ppermute | solution.py:800
  154.6 9.4 %copy-start.10 = (bf16[768,512]{1,0:T(8,128)(2,1)}, bf16[768,512]{1,0:T(8,128)(2,1)S(1)}, u32[]{:S(2)}) copy-start(bf16[768,512]{1,0:T(8,128)(2,1)S(1)} %constant_dynamic-update-slice_fusion.refs_7_.refs_13_) | copy-start | bytes 2359300
  164.0 38.2 %copy-start.3 = (bf16[512,512]{1,0:T(8,128)(2,1)S(1)}, bf16[512,512]{1,0:T(8,128)(2,1)}, u32[]{:S(2)}) copy-start(bf16[512,512]{1,0:T(8,128)(2,1)} %get-tuple-element.89) | copy-start | bytes 1572868
  201.9 32.6 %collective-permute-start.5 = (bf16[8,256,512]{2,1,0:T(8,128)(2,1)}, bf16[8,256,512]{2,1,0:T(8,128)(2,1)}, u32[]{:S(2)}, u32[]{:S(2)}) collective-permute-start(bf16[8,256,512]{2,1,0:T(8,128)(2,1)} %get-tuple-element.128), channel_id=1, source_target_pairs={{0,1},{1,0},{2,3},{3,2},{4,5},{5,4},{6,7},{7,6},{8,9},{9,8},{10,11... | collective-permute-start | bytes 6291464 | tf_op jit(solution)/shard_map/ppermute | solution.py:839
  202.2 6.1 %copy-start.38 = (bf16[256,512]{1,0:T(8,128)(2,1)S(1)}, bf16[256,512]{1,0:T(8,128)(2,1)}, u32[]{:S(2)}) copy-start(bf16[256,512]{1,0:T(8,128)(2,1)} %get-tuple-element.110) | copy-start | bytes 786436
  204.4 28.8 %all-to-all-start.1 = ((bf16[4,2,128,512]{3,2,1,0:T(8,128)(2,1)}), bf16[4,2,128,512]{3,2,1,0:T(8,128)(2,1)S(1)}, u32[]{:S(2)}, u32[]{:S(2)}) async-start(bf16[4,2,128,512]{3,2,1,0:T(8,128)(2,1)} %maximum_bitcast_fusion), calls=%async_computation.1 | async-start | bytes 2097152 | tf_op jit(solution)/shard_map/all_to_all | solution.py:1000
  208.3 23.7 %collective-permute-start.4 = (bf16[256,512]{1,0:T(8,128)(2,1)S(1)}, bf16[256,512]{1,0:T(8,128)(2,1)S(1)}, u32[]{:S(2)}, u32[]{:S(2)}) collective-permute-start(bf16[256,512]{1,0:T(8,128)(2,1)S(1)} %copy-done.38), channel_id=1, source_target_pairs={{0,16},{16,0},{1,17},{17,1},{2,18},{18,2},{3,19},{19,3},{4,20},{20... | collective-permute-start | bytes 786440 | tf_op jit(solution)/shard_map/ppermute | solution.py:800
  232.0 6.9 %copy-start.16 = (bf16[256,512]{1,0:T(8,128)(2,1)}, bf16[256,512]{1,0:T(8,128)(2,1)S(1)}, u32[]{:S(2)}) copy-start(bf16[256,512]{1,0:T(8,128)(2,1)S(1)} %collective-permute-done.4.refs_21_) | copy-start | bytes 786436
  238.9 36.0 %all-to-all-start.2 = ((bf16[8,256,512]{2,1,0:T(8,128)(2,1)}), bf16[8,256,512]{2,1,0:T(8,128)(2,1)S(1)}, u32[]{:S(2)}, u32[]{:S(2)}) async-start(bf16[8,256,512]{2,1,0:T(8,128)(2,1)} %add_convert_fusion.1.refs_20_), calls=%async_computation.2 | async-start | bytes 4194304 | tf_op jit(solution)/shard_map/all_to_all | solution.py:874
  243.9 16.0 %copy-start.37 = (bf16[256,512]{1,0:T(8,128)(2,1)S(1)}, bf16[256,512]{1,0:T(8,128)(2,1)}, u32[]{:S(2)}) copy-start(bf16[256,512]{1,0:T(8,128)(2,1)} %get-tuple-element.130) | copy-start | bytes 786436
  259.8 16.6 %collective-permute-start.7 = (bf16[8,192,512]{2,1,0:T(8,128)(2,1)}, bf16[8,192,512]{2,1,0:T(8,128)(2,1)}, u32[]{:S(2)}, u32[]{:S(2)}) collective-permute-start(bf16[8,192,512]{2,1,0:T(8,128)(2,1)} %get-tuple-element.131), channel_id=1, source_target_pairs={{0,1},{1,0},{2,3},{3,2},{4,5},{5,4},{6,7},{7,6},{8,9},{9,8},{10,11... | collective-permute-start | bytes 4718600 | tf_op jit(solution)/shard_map/ppermute | solution.py:839
  259.9 13.1 %collective-permute-start.6 = (bf16[256,512]{1,0:T(8,128)(2,1)S(1)}, bf16[256,512]{1,0:T(8,128)(2,1)S(1)}, u32[]{:S(2)}, u32[]{:S(2)}) collective-permute-start(bf16[256,512]{1,0:T(8,128)(2,1)S(1)} %copy-done.37), channel_id=1, source_target_pairs={{0,16},{16,0},{1,17},{17,1},{2,18},{18,2},{3,19},{19,3},{4,20},{20... | collective-permute-start | bytes 786440 | tf_op jit(solution)/shard_map/ppermute | solution.py:800
  279.6 6.4 %copy-start.17 = (bf16[256,512]{1,0:T(8,128)(2,1)S(1)}, bf16[256,512]{1,0:T(8,128)(2,1)}, u32[]{:S(2)}) copy-start(bf16[256,512]{1,0:T(8,128)(2,1)} %copy-done.16) | copy-start | bytes 786436
  279.6 27.1 %all-to-all-start.3 = ((bf16[8,192,512]{2,1,0:T(8,128)(2,1)}), bf16[8,192,512]{2,1,0:T(8,128)(2,1)S(1)}, u32[]{:S(2)}, u32[]{:S(2)}) async-start(bf16[8,192,512]{2,1,0:T(8,128)(2,1)} %add_convert_fusion.3.refs_12_), calls=%async_computation.3 | async-start | bytes 3145728 | tf_op jit(solution)/shard_map/all_to_all | solution.py:874
  306.6 4.6 %collective-permute-start.8 = (bf16[8,256,512]{2,1,0:T(8,128)(2,1)}, bf16[8,256,512]{2,1,0:T(8,128)(2,1)}, u32[]{:S(2)}, u32[]{:S(2)}) collective-permute-start(bf16[8,256,512]{2,1,0:T(8,128)(2,1)} %get-tuple-element.146), channel_id=1, source_target_pairs={{0,1},{1,0},{2,3},{3,2},{4,5},{5,4},{6,7},{7,6},{8,9},{9,8},{10,11... | collective-permute-start | bytes 6291464 | tf_op jit(solution)/shard_map/ppermute | solution.py:839
  315.4 32.8 %all-to-all-start.6 = ((bf16[8,256,512]{2,1,0:T(8,128)(2,1)}), bf16[8,256,512]{2,1,0:T(8,128)(2,1)S(1)}, u32[]{:S(2)}, u32[]{:S(2)}) async-start(bf16[8,256,512]{2,1,0:T(8,128)(2,1)} %add_convert_fusion.refs_23_), calls=%async_computation.6 | async-start | bytes 4194304 | tf_op jit(solution)/shard_map/all_to_all | solution.py:874
  336.7 3.9 collective-permute-start.10
  348.3 38.0 %all-to-all-start.4 = ((bf16[8,208,512]{2,1,0:T(8,128)(2,1)}), bf16[8,208,512]{2,1,0:T(8,128)(2,1)}, u32[]{:S(2)}, u32[]{:S(2)}) async-start(bf16[8,208,512]{2,1,0:T(8,128)(2,1)} %add_convert_fusion.2), calls=%async_computation.4 | async-start | bytes 3407872 | tf_op jit(solution)/shard_map/all_to_all | solution.py:874
  355.5 23.9 %copy-start.7 = (f32[128,512]{1,0:T(8,128)S(1)}, f32[128,512]{1,0:T(8,128)}, u32[]{:S(2)}) copy-start(f32[128,512]{1,0:T(8,128)} %param.22) | copy-start | bytes 786436
  355.6 23.9 %copy-start.25 = (f32[128,512]{1,0:T(8,128)S(1)}, f32[128,512]{1,0:T(8,128)}, u32[]{:S(2)}) copy-start(f32[128,512]{1,0:T(8,128)} %param.26) | copy-start | bytes 786436
  355.6 23.9 %copy-start.26 = (f32[128,512]{1,0:T(8,128)S(1)}, f32[128,512]{1,0:T(8,128)}, u32[]{:S(2)}) copy-start(f32[128,512]{1,0:T(8,128)} %param.30) | copy-start | bytes 786436
  355.6 23.7 %collective-permute-start.12 = (bf16[256,512]{1,0:T(8,128)(2,1)S(1)}, bf16[256,512]{1,0:T(8,128)(2,1)S(1)}, u32[]{:S(2)}, u32[]{:S(2)}) collective-permute-start(bf16[256,512]{1,0:T(8,128)(2,1)S(1)} %select_convert_fusion), channel_id=1, source_target_pairs={{0,16},{16,0},{1,17},{17,1},{2,18},{18,2},{3,19},{19,3},{4,20},{20... | collective-permute-start | bytes 786440 | tf_op jit(solution)/shard_map/ppermute | solution.py:800
  357.8 22.8 %copy-start.9 = (f32[32,2048]{1,0:T(8,128)S(1)}, f32[32,2048]{1,0:T(8,128)}, u32[]{:S(2)}) copy-start(f32[32,2048]{1,0:T(8,128)} %param.21) | copy-start | bytes 786436
  357.8 22.8 %copy-start.27 = (f32[32,2048]{1,0:T(8,128)S(1)}, f32[32,2048]{1,0:T(8,128)}, u32[]{:S(2)}) copy-start(f32[32,2048]{1,0:T(8,128)} %param.25) | copy-start | bytes 786436
  357.8 22.7 %copy-start.28 = (f32[32,2048]{1,0:T(8,128)S(1)}, f32[32,2048]{1,0:T(8,128)}, u32[]{:S(2)}) copy-start(f32[32,2048]{1,0:T(8,128)} %param.29) | copy-start | bytes 786436
  357.8 31.4 %collective-permute-start.9 = (bf16[256,512]{1,0:T(8,128)(2,1)}, bf16[256,512]{1,0:T(8,128)(2,1)}, u32[]{:S(2)}, u32[]{:S(2)}) collective-permute-start(bf16[256,512]{1,0:T(8,128)(2,1)} %get-tuple-element.148), channel_id=1, source_target_pairs={{0,16},{16,0},{1,17},{17,1},{2,18},{18,2},{3,19},{19,3},{4,20},{20... | collective-permute-start | bytes 786440 | tf_op jit(solution)/shard_map/ppermute | solution.py:800
  380.5 8.7 %copy-start.21 = (f32[4,4,8,512]{3,2,0,1:T(8,128)}, f32[4,4,8,512]{3,2,0,1:T(8,128)S(1)}, u32[]{:S(2)}) copy-start(f32[4,4,8,512]{3,2,0,1:T(8,128)S(1)} %copy.85) | copy-start | bytes 786436
  391.8 21.7 %all-to-all-start.5 = ((bf16[4,2,128,512]{3,2,1,0:T(8,128)(2,1)}), bf16[4,2,128,512]{3,2,1,0:T(8,128)(2,1)S(1)}, u32[]{:S(2)}, u32[]{:S(2)}) async-start(bf16[4,2,128,512]{3,2,1,0:T(8,128)(2,1)} %maximum_bitcast_fusion.1), calls=%async_computation.5 | async-start | bytes 2097152 | tf_op jit(solution)/shard_map/all_to_all | solution.py:1000
  395.4 16.0 %copy-start.23 = (f32[192,512]{1,0:T(8,128)S(1)}, f32[192,512]{1,0:T(8,128)}, u32[]{:S(2)}) copy-start(f32[192,512]{1,0:T(8,128)} %param.24) | copy-start | bytes 1179652
  395.4 16.0 %copy-start.24 = (f32[192,512]{1,0:T(8,128)S(1)}, f32[192,512]{1,0:T(8,128)}, u32[]{:S(2)}) copy-start(f32[192,512]{1,0:T(8,128)} %param.28) | copy-start | bytes 1179652
  395.5 15.8 %collective-permute-start.11 = (bf16[208,512]{1,0:T(8,128)(2,1)S(1)}, bf16[208,512]{1,0:T(8,128)(2,1)S(1)}, u32[]{:S(2)}, u32[]{:S(2)}) collective-permute-start(bf16[208,512]{1,0:T(8,128)(2,1)S(1)} %select_convert_fusion.1), channel_id=1, source_target_pairs={{0,16},{16,0},{1,17},{17,1},{2,18},{18,2},{3,19},{19,3},{4,20},{20... | collective-permute-start | bytes 638984 | tf_op jit(solution)/shard_map/ppermute | solution.py:800
  395.8 16.8 %copy-start.32 = (f32[160]{0:T(256)S(1)}, f32[160]{0:T(256)}, u32[]{:S(2)}) copy-start(f32[160]{0:T(256)} %param.23) | copy-start | bytes 1924
  395.8 16.8 %copy-start.35 = (f32[160]{0:T(256)S(1)}, f32[160]{0:T(256)}, u32[]{:S(2)}) copy-start(f32[160]{0:T(256)} %param.27) | copy-start | bytes 1924
  395.9 16.8 %copy-start.36 = (f32[160]{0:T(256)S(1)}, f32[160]{0:T(256)}, u32[]{:S(2)}) copy-start(f32[160]{0:T(256)} %param.31) | copy-start | bytes 1924
  412.5 20.5 %copy-start.13 = (f32[192,512]{1,0:T(8,128)}, f32[192,512]{1,0:T(8,128)S(1)}, u32[]{:S(2)}) copy-start(f32[192,512]{1,0:T(8,128)S(1)} %get-tuple-element.174) | copy-start | bytes 1179652
  412.5 20.5 %copy-start.14 = (f32[192,512]{1,0:T(8,128)}, f32[192,512]{1,0:T(8,128)S(1)}, u32[]{:S(2)}) copy-start(f32[192,512]{1,0:T(8,128)S(1)} %get-tuple-element.175) | copy-start | bytes 1179652
  412.5 17.7 %copy-start.19 = (f32[128,512]{1,0:T(8,128)S(1)}, f32[128,512]{1,0:T(8,128)}, u32[]{:S(2)}) copy-start(f32[128,512]{1,0:T(8,128)} %get-tuple-element.179) | copy-start | bytes 786436
  412.5 17.7 %copy-start.20 = (f32[128,512]{1,0:T(8,128)S(1)}, f32[128,512]{1,0:T(8,128)}, u32[]{:S(2)}) copy-start(f32[128,512]{1,0:T(8,128)} %get-tuple-element.180) | copy-start | bytes 786436
  415.4 13.1 %all-to-all-start.7 = ((f32[32,8,128]{2,1,0:T(8,128)}), f32[32,8,128]{2,1,0:T(8,128)S(1)}, u32[]{:S(2)}, u32[]{:S(2)}) async-start(f32[32,8,128]{2,1,0:T(8,128)} %broadcast_in_dim.170), calls=%async_computation.7 | async-start | bytes 262144 | tf_op jit(solution)/shard_map/all_to_all | solution.py:1061
  (14 other events, 51.9 us)
Sparse Core Ops, SparseCore 0:
  49.3 71.0 all-gather.4
  122.6 41.3 all-gather.6
where the time goes:
time: 446 us; the launch traced here: 441 us
  waiting for transfers between devices  166 us (37%)
  Pallas kernels  136 us (30%)
  starting transfers between devices  54.4 us (12%)
  other arithmetic  48.6 us (11%)
  between operations  21.1 us (5%)
  local copies, waits for them, and re-layouts  14.9 us (3%)
    pallas_call x7, Pallas kernels, fused(): pl.pallas_call(body, in_specs=[pl.BlockSpec(memory_space=pltpu.SMEM)] + [...  136 us
    ppermute x9, waiting for transfers between devices, swap_hi(): return lax.ppermute(array, 'hi', [(0, 1), (1, 0)])  90.5 us
    all_gather x1, waiting for transfers between devices, shards(): full = lax.all_gather(early, GROUP, axis=0, tiled=False)  43.4 us
    all_to_all x4, starting transfers between devices, reduce_chips(): parts = lax.all_to_all(pair, CHIPS, split_axis=0, concat_axis=0, tiled=True)  21.2 us
    convert_element_type x4, other arithmetic, reduce_cores(): return (kept.astype(F32) + swap_core(sent).astype(F32)).astype(BF)  15.1 us
    ppermute x9, starting transfers between devices, swap_hi(): return lax.ppermute(array, 'hi', [(0, 1), (1, 0)])  15 us
    all_to_all x4, waiting for transfers between devices, reduce_chips(): parts = lax.all_to_all(pair, CHIPS, split_axis=0, concat_axis=0, tiled=True)  9.65 us
    all_gather x1, waiting for transfers between devices, shards(): late = lax.all_gather(one[attn_rows:last], GROUP, axis=0, tiled=False)  9.36 us
  transfers between devices with their start and end apart: 23, of which 14 were waited for; matrix products, arithmetic and copies ran while one was open for 8% of the time, Pallas kernels for 22%

commit v1 on v0

--- a/solution.py
+++ b/solution.py
@@ -1012,13 +1012,13 @@
         pair_a1 = sb.kept
     else:
         part_f1 = reduce_chips(pair_f1)
-        pair_a1 = reduce_cores(tie(tie(sb.kept, part_f1), back_s), sb.sent)
+        pair_a1 = reduce_cores(tie(sb.kept, part_f1), sb.sent)
     eh = enc_ffn_head(grad_encoded, e.resid, e.two, e, pack0, mats[0:4], gains, places, (pair_a1,))
     if plain:
         pair_f0 = eh.kept
     else:
         part_a1 = reduce_chips(pair_a1)
-        pair_f0 = reduce_cores(tie(eh.kept, part_a1), eh.sent)
+        pair_f0 = reduce_cores(tie(tie(eh.kept, part_a1), back_s), eh.sent)
     eb = input_body(
         "enc_body", e, eh, enc_rows, enc_window, mats[0:4], False, eh.late, ("q", "k", "v", 0, 1, 2),
         (eh.dwo, sb.dwq, sb.dwk), (eh.ng, eh.ng2, sh.ng, c.ng, c.ng8), group, places, (pair_f0,),

time: 446 us -> 451 us (1.011)
  waiting for transfers between devices: 166 us -> 172 us
    all_to_all x4, waiting for transfers between devices: 9.65 us -> 17.6 us  [reduce_chips(): parts = lax.all_to_all(pair, CHIPS, split_axis=0, concat_axis=0, tiled=True)]
where the time goes in v1:
time: 451 us; the launch traced here: 446 us
  waiting for transfers between devices  172 us (38%)
  Pallas kernels  136 us (30%)
  starting transfers between devices  54.5 us (12%)
  other arithmetic  48.6 us (11%)
  between operations  21.1 us (5%)
  local copies, waits for them, and re-layouts  14.7 us (3%)
    pallas_call x7, Pallas kernels, fused(): pl.pallas_call(body, in_specs=[pl.BlockSpec(memory_space=pltpu.SMEM)] + [...  136 us
    ppermute x9, waiting for transfers between devices, swap_hi(): return lax.ppermute(array, 'hi', [(0, 1), (1, 0)])  90.2 us
    all_gather x1, waiting for transfers between devices, shards(): full = lax.all_gather(early, GROUP, axis=0, tiled=False)  43.4 us
    all_to_all x4, starting transfers between devices, reduce_chips(): parts = lax.all_to_all(pair, CHIPS, split_axis=0, concat_axis=0, tiled=True)  19.2 us
    all_to_all x4, waiting for transfers between devices, reduce_chips(): parts = lax.all_to_all(pair, CHIPS, split_axis=0, concat_axis=0, tiled=True)  17.6 us
    ppermute x9, starting transfers between devices, swap_hi(): return lax.ppermute(array, 'hi', [(0, 1), (1, 0)])  17 us
    convert_element_type x4, other arithmetic, reduce_cores(): return (kept.astype(F32) + swap_core(sent).astype(F32)).astype(BF)  15.1 us
    all_gather x1, waiting for transfers between devices, shards(): late = lax.all_gather(one[attn_rows:last], GROUP, axis=0, tiled=False)  9.36 us
  transfers between devices with their start and end apart: 23, of which 14 were waited for; matrix products, arithmetic and copies ran while one was open for 8% of the time, Pallas kernels for 22%

profile of v1, /device:TPU:0, one launch (start us, length us, event | category | flops | bytes accessed | tf_op | source)
XLA Modules:
  0.0 446.2 jit_solution(10588478415701619408)
XLA Ops:
  7.2 2.7 pad_maximum_fusion
  9.9 5.4 %all-to-all-start = ((bf16[4,3,128,512]{3,2,1,0:T(8,128)(2,1)}), bf16[4,3,128,512]{3,2,1,0:T(8,128)(2,1)S(1)}, u32[]{:S(2)}, u32[]{:S(2)}) async-start(bf16[4,3,128,512]{3,2,1,0:T(8,128)(2,1)} %pad_maximum_fusion), calls=%async_computation | async-start | bytes 3145728 | tf_op jit(solution)/shard_map/all_to_all | solution.py:938
  15.6 2.7 collective-permute-start
  18.2 24.3 %collective-permute-done = bf16[464,512]{1,0:T(8,128)(2,1)} collective-permute-done((bf16[464,512]{1,0:T(8,128)(2,1)S(1)}, bf16[464,512]{1,0:T(8,128)(2,1)}, u32[]{:S(2)}, u32[]{:S(2)}) %collective-permute-start) | collective-permute-done | bytes 475168 | tf_op jit(solution)/shard_map/ppermute | solution.py:800
  42.5 1.2 broadcast_select_fusion.1
  50.5 3.6 collective-permute-start.1
  56.8 13.6 %collective-permute-done.1 = bf16[256,512]{1,0:T(8,128)(2,1)S(1)} collective-permute-done((bf16[256,512]{1,0:T(8,128)(2,1)S(1)}, bf16[256,512]{1,0:T(8,128)(2,1)S(1)}, u32[]{:S(2)}, u32[]{:S(2)}) %collective-permute-start.1) | collective-permute-done | bytes 262176 | tf_op jit(solution)/shard_map/ppermute | solution.py:800
  71.3 4.8 %collective-permute-done.2 = bf16[256,512]{1,0:T(8,128)(2,1)S(1)} collective-permute-done((bf16[256,512]{1,0:T(8,128)(2,1)S(1)}, bf16[256,512]{1,0:T(8,128)(2,1)S(1)}, u32[]{:S(2)}, u32[]{:S(2)}) %collective-permute-start.2) | collective-permute-done | bytes 262176 | tf_op jit(solution)/shard_map/ppermute | solution.py:800
  77.1 43.4 %all-gather.5.cloned.1.call-done = bf16[10496,512]{1,0:T(8,128)(2,1)} async-done(((bf16[656,512]{1,0:T(8,128)(2,1)}), bf16[10496,512]{1,0:T(8,128)(2,1)}) %all-gather.5.cloned.1.call-update) | async-done | bytes 10747920 | tf_op jit(solution)/shard_map/all_gather | solution.py:960
  122.0 15.3 %enc_forward.1 = (bf16[512,512]{1,0:T(8,128)(2,1)}, bf16[768,512]{1,0:T(8,128)(2,1)}, bf16[768,512]{1,0:T(8,128)(2,1)}, f32[8,512]{1,0:T(8,128)}, bf16[512,512]{...) custom-call(s32[2]{0:T(128)} %pad_add_fusion.3.core_ref, ...), custom_call_target="tpu_custom_call" | custom-call | flops 5368709120 | bytes 12058624 | tf_op jit(solution)/shard_map/enc_forward/pallas_call | solution.py:178
  138.4 2.2 collective-permute-start.3
  141.7 12.9 %self_forward.1 = (bf16[512,512]{1,0:T(8,128)(2,1)}, bf16[768,512]{1,0:T(8,128)(2,1)}, bf16[768,512]{1,0:T(8,128)(2,1)}, f32[8,512]{1,0:T(8,128)}, bf16[512,512]{1,0:T(8,128)(2,1)}, /*index=5*/f32[512,512]{1,0:T(8,128)}) custom-call(s32[2]{0:T(128)} %pad_add_fusion.3.core_ref, s32[512,2]{1,0:T(8,128)} %slice.183.refs_0_, s32[2,768]{1,0:T(2,128)} %pad_add_fusion.refs_1_, ...), custom_call_target="tpu_custom_call" | custom-call | flops 3221225472 | bytes 12058624 | tf_op jit(solution)/shard_map/self_forward/pallas_call | solution.py:178
  154.7 9.4 %all-gather.7.cloned.1.call-done = bf16[4096,512]{1,0:T(8,128)(2,1)} async-done(((bf16[256,512]{1,0:T(8,128)(2,1)}), bf16[4096,512]{1,0:T(8,128)(2,1)}) %all-gather.7.cloned.1.call-update) | async-done | bytes 4194320 | tf_op jit(solution)/shard_map/all_gather | solution.py:961
  164.0 37.9 %cross_and_ffn.1 = (bf16[512,512]{1,0:T(8,128)(2,1)}, bf16[768,512]{1,0:T(8,128)(2,1)}, bf16[768,512]{1,0:T(8,128)(2,1)}, f32[8,512]{1,0:T(8,128)}, bf16[512,512...) custom-call(s32[2]{0:T(128)} %pad_add_fusion.3.core_ref, ...), custom_call_target="tpu_custom_call" | custom-call | flops 10737418240 | bytes 17825792 | tf_op jit(solution)/shard_map/cross_and_ffn/pallas_call | solution.py:178
  202.3 2.2 maximum_bitcast_fusion
  204.4 3.9 all-to-all-start.1
  208.4 2.3 collective-permute-start.4
  210.7 19.5 %cross_body_self_head.1 = (f32[512,512]{1,0:T(8,128)}, bf16[512,512]{1,0:T(8,128)(2,1)}, bf16[512,512]{1,0:T(8,128)(2,1)}, bf16[512,512]{1,0:T(8,128)(2,1)}, f32...) custom-call(s32[2]{0:T(128)} %pad_add_fusion.3.core_ref, ...), custom_call_target="tpu_custom_call" | custom-call | flops 4429185024 | bytes 19972096 | tf_op jit(solution)/shard_map/cross_body_self_head/pallas_call | solution.py:178
  230.2 1.2 slice.157
  234.5 4.4 add_convert_fusion.1.refs_20_
  238.9 5.0 %all-to-all-start.2 = ((bf16[8,256,512]{2,1,0:T(8,128)(2,1)}), bf16[8,256,512]{2,1,0:T(8,128)(2,1)S(1)}, u32[]{:S(2)}, u32[]{:S(2)}) async-start(bf16[8,256,512]{2,1,0:T(8,128)(2,1)} %add_convert_fusion.1.refs_20_), calls=%async_computation.2 | async-start | bytes 4194304 | tf_op jit(solution)/shard_map/all_to_all | solution.py:874
  243.9 15.8 %self_body.1 = (bf16[8,192,512]{2,1,0:T(8,128)(2,1)}, bf16[8,192,512]{2,1,0:T(8,128)(2,1)}, bf16[512,512]{1,0:T(8,128)(2,1)}, bf16[512,512]{1,0:T(8,128)(2,1)}, f32[512,512]{1,0:T(8,128)}) custom-call(s32[2]{0:T(128)} %pad_add_fusion.3.core_ref, s32[2,512]{1,0:T(2,128)} %fusion.6.refs_2_.refs_0_, s32[768,2]{1,0:T(8,128)} %copy-done, ...), custom_call_target="tpu_custom_call" | custom-call | flops 3221225472 | bytes 20480000 | tf_op jit(solution)/shard_map/self_body/pallas_call | solution.py:178
  259.8 9.9 %all-to-all-done.2 = bf16[8,256,512]{2,1,0:T(8,128)(2,1)S(1)} async-done(((bf16[8,256,512]{2,1,0:T(8,128)(2,1)}), bf16[8,256,512]{2,1,0:T(8,128)(2,1)S(1)}, u32[]{:S(2)}, u32[]{:S(2)}) %all-to-all-start.2) | async-done | bytes 2097184 | tf_op jit(solution)/shard_map/all_to_all | solution.py:874
  271.2 3.1 add_convert_fusion.3.refs_12_
  274.4 5.0 %all-to-all-start.3 = ((bf16[8,192,512]{2,1,0:T(8,128)(2,1)}), bf16[8,192,512]{2,1,0:T(8,128)(2,1)S(1)}, u32[]{:S(2)}, u32[]{:S(2)}) async-start(bf16[8,192,512]{2,1,0:T(8,128)(2,1)} %add_convert_fusion.3.refs_12_), calls=%async_computation.3 | async-start | bytes 3145728 | tf_op jit(solution)/shard_map/all_to_all | solution.py:874
  279.4 2.3 convert_add_fusion.refs_5_
  281.8 18.3 %enc_ffn_head.1 = (bf16[8,256,512]{2,1,0:T(8,128)(2,1)}, bf16[8,256,512]{2,1,0:T(8,128)(2,1)}, f32[512,512]{1,0:T(8,128)}, f32[2,512]{1,0:T(2,128)}, f32[512,512...) custom-call(s32[2]{0:T(128)} %pad_add_fusion.3.core_ref, ...), custom_call_target="tpu_custom_call" | custom-call | flops 6241124352 | bytes 16531456 | tf_op jit(solution)/shard_map/enc_ffn_head/pallas_call | solution.py:178
  300.2 1.7 collective-permute-start.7
  301.8 13.6 %collective-permute-done.7 = bf16[256,512]{1,0:T(8,128)(2,1)S(1)} collective-permute-done((bf16[256,512]{1,0:T(8,128)(2,1)S(1)}, bf16[256,512]{1,0:T(8,128)(2,1)S(1)}, u32[]{:S(2)}, u32[]{:S(2)}) %collective-permute-start.7) | collective-permute-done | bytes 262176 | tf_op jit(solution)/shard_map/ppermute | solution.py:800
  318.0 4.4 add_convert_fusion.refs_23_
  322.4 4.4 all-to-all-start.6
  326.8 16.0 %enc_body.1 = (bf16[8,208,512]{2,1,0:T(8,128)(2,1)}, bf16[8,208,512]{2,1,0:T(8,128)(2,1)}, bf16[512,512]{1,0:T(8,128)(2,1)}, bf16[512,512]{1,0:T(8,128)(2,1)}, f32[512,512]{1,0:T(8,128)}) custom-call(s32[2]{0:T(128)} %pad_add_fusion.3.core_ref, s32[2,512]{1,0:T(2,128)} %fusion.6.refs_2_.refs_0_, s32[768,2]{1,0:T(8,128)} %copy-done, ...), custom_call_target="tpu_custom_call" | custom-call | flops 3221225472 | bytes 19451904 | tf_op jit(solution)/shard_map/enc_body/pallas_call | solution.py:178
  342.8 3.8 collective-permute-done.10
  346.6 3.2 add_convert_fusion.2
  349.8 3.1 all-to-all-done.6
  352.9 4.8 %all-to-all-start.4 = ((bf16[8,208,512]{2,1,0:T(8,128)(2,1)}), bf16[8,208,512]{2,1,0:T(8,128)(2,1)}, u32[]{:S(2)}, u32[]{:S(2)}) async-start(bf16[8,208,512]{2,1,0:T(8,128)(2,1)} %add_convert_fusion.2), calls=%async_computation.4 | async-start | bytes 3407872 | tf_op jit(solution)/shard_map/all_to_all | solution.py:874
  357.8 2.2 fusion.19
  360.5 3.3 collective-permute-start.12
  364.9 19.4 %collective-permute-done.12 = bf16[256,512]{1,0:T(8,128)(2,1)S(1)} collective-permute-done((bf16[256,512]{1,0:T(8,128)(2,1)S(1)}, bf16[256,512]{1,0:T(8,128)(2,1)S(1)}, u32[]{:S(2)}, u32[]{:S(2)}) %collective-permute-start.12) | collective-permute-done | bytes 262176 | tf_op jit(solution)/shard_map/ppermute | solution.py:800
  386.7 4.6 %all-to-all-done.4 = bf16[8,208,512]{2,1,0:T(8,128)(2,1)} async-done(((bf16[8,208,512]{2,1,0:T(8,128)(2,1)}), bf16[8,208,512]{2,1,0:T(8,128)(2,1)}, u32[]{:S(2)}, u32[]{:S(2)}) %all-to-all-start.4) | async-done | bytes 1703968 | tf_op jit(solution)/shard_map/all_to_all | solution.py:874
  391.3 1.7 convert_reduce_fusion.2
  394.2 1.5 fusion.1
  396.8 4.1 all-to-all-start.5
  401.9 14.5 %collective-permute-done.11 = bf16[208,512]{1,0:T(8,128)(2,1)S(1)} collective-permute-done((bf16[208,512]{1,0:T(8,128)(2,1)S(1)}, bf16[208,512]{1,0:T(8,128)(2,1)S(1)}, u32[]{:S(2)}, u32[]{:S(2)}) %collective-permute-start.11) | collective-permute-done | bytes 213024 | tf_op jit(solution)/shard_map/ppermute | solution.py:800
  421.1 4.2 all-to-all-start.7
  425.4 1.6 slice_convert_fusion
  427.0 6.6 %all-to-all-done.7 = f32[32,8,128]{2,1,0:T(8,128)S(1)} async-done(((f32[32,8,128]{2,1,0:T(8,128)}), f32[32,8,128]{2,1,0:T(8,128)S(1)}, u32[]{:S(2)}, u32[]{:S(2)}) %all-to-all-start.7) | async-done | bytes 131104 | tf_op jit(solution)/shard_map/all_to_all | solution.py:1061
  436.2 1.9 fusion.11
  (192 shorter events, 32.2 us)
Async XLA Ops:
  9.9 35.3 %all-to-all-start = ((bf16[4,3,128,512]{3,2,1,0:T(8,128)(2,1)}), bf16[4,3,128,512]{3,2,1,0:T(8,128)(2,1)S(1)}, u32[]{:S(2)}, u32[]{:S(2)}) async-start(bf16[4,3,128,512]{3,2,1,0:T(8,128)(2,1)} %pad_maximum_fusion), calls=%async_computation | async-start | bytes 3145728 | tf_op jit(solution)/shard_map/all_to_all | solution.py:938
  15.3 105.2 %all-gather.5.cloned.1.call-start = ((), (), s32[]{:S(2)}) async-start(), calls=%async_computation.8 | async-start | bytes 11419648 | tf_op jit(solution)/shard_map/all_gather | solution.py:960
  15.6 26.9 %collective-permute-start = (bf16[464,512]{1,0:T(8,128)(2,1)S(1)}, bf16[464,512]{1,0:T(8,128)(2,1)}, u32[]{:S(2)}, u32[]{:S(2)}) collective-permute-start(bf16[464,512]{1,0:T(8,128)(2,1)S(1)} %fusion.2), channel_id=1, source_target_pairs={{0,16},{16,0},{1,17},{17,1},{2,18},{18,2},{3,19},{19,3},{4,20},{20... | collective-permute-start | bytes 1425416 | tf_op jit(solution)/shard_map/ppermute | solution.py:800
  46.2 24.3 %copy-start.2 = (bf16[1,4,128,512]{3,2,0,1:T(8,128)(2,1)}, bf16[1,4,128,512]{3,2,0,1:T(8,128)(2,1)S(1)}, u32[]{:S(2)}) copy-start(bf16[1,4,128,512]{3,2,0,1:T(8,128)(2,1)S(1)} %get-tuple-element.189) | copy-start | bytes 1572868
  46.2 30.0 %copy-start.1 = (bf16[1,4,128,512]{3,2,0,1:T(8,128)(2,1)}, bf16[1,4,128,512]{3,2,0,1:T(8,128)(2,1)S(1)}, u32[]{:S(2)}) copy-start(bf16[1,4,128,512]{3,2,0,1:T(8,128)(2,1)S(1)} %get-tuple-element.188) | copy-start | bytes 1572868
  49.2 114.8 %all-gather.7.cloned.1.call-start = ((), (), s32[]{:S(2)}) async-start(), calls=%async_computation.9 | async-start | bytes 4456448 | tf_op jit(solution)/shard_map/all_gather | solution.py:961
  50.5 19.9 %collective-permute-start.1 = (bf16[256,512]{1,0:T(8,128)(2,1)S(1)}, bf16[256,512]{1,0:T(8,128)(2,1)S(1)}, u32[]{:S(2)}, u32[]{:S(2)}) collective-permute-start(bf16[256,512]{1,0:T(8,128)(2,1)S(1)} %bitcast.99), channel_id=1, source_target_pairs={{0,16},{16,0},{1,17},{17,1},{2,18},{18,2},{3,19},{19,3},{4,20},{20... | collective-permute-start | bytes 786440 | tf_op jit(solution)/shard_map/ppermute | solution.py:800
  54.7 21.5 %collective-permute-start.2 = (bf16[256,512]{1,0:T(8,128)(2,1)S(1)}, bf16[256,512]{1,0:T(8,128)(2,1)S(1)}, u32[]{:S(2)}, u32[]{:S(2)}) collective-permute-start(bf16[256,512]{1,0:T(8,128)(2,1)S(1)} %bitcast.98), channel_id=1, source_target_pairs={{0,16},{16,0},{1,17},{17,1},{2,18},{18,2},{3,19},{19,3},{4,20},{20... | collective-permute-start | bytes 786440 | tf_op jit(solution)/shard_map/ppermute | solution.py:800
  55.4 81.9 %copy-start = (s32[768,2]{1,0:T(8,128)}, s32[768,2]{1,0:T(8,128)S(1)}, u32[]{:S(2)}) copy-start(s32[768,2]{1,0:T(8,128)S(1)} %copy.72.refs_3_.refs_1_) | copy-start | bytes 18436
  138.4 16.2 %collective-permute-start.3 = (bf16[256,512]{1,0:T(8,128)(2,1)S(1)}, bf16[256,512]{1,0:T(8,128)(2,1)S(1)}, u32[]{:S(2)}, u32[]{:S(2)}) collective-permute-start(bf16[256,512]{1,0:T(8,128)(2,1)S(1)} %slice_select_fusion.2), channel_id=1, source_target_pairs={{0,16},{16,0},{1,17},{17,1},{2,18},{18,2},{3,19},{19,3},{4,20},{20... | collective-permute-start | bytes 786440 | tf_op jit(solution)/shard_map/ppermute | solution.py:800
  154.7 9.4 %copy-start.10 = (bf16[768,512]{1,0:T(8,128)(2,1)}, bf16[768,512]{1,0:T(8,128)(2,1)S(1)}, u32[]{:S(2)}) copy-start(bf16[768,512]{1,0:T(8,128)(2,1)S(1)} %constant_dynamic-update-slice_fusion.refs_7_.refs_13_) | copy-start | bytes 2359300
  164.0 38.2 %copy-start.3 = (bf16[512,512]{1,0:T(8,128)(2,1)S(1)}, bf16[512,512]{1,0:T(8,128)(2,1)}, u32[]{:S(2)}) copy-start(bf16[512,512]{1,0:T(8,128)(2,1)} %get-tuple-element.89) | copy-start | bytes 1572868
  201.9 32.6 %collective-permute-start.5 = (bf16[8,256,512]{2,1,0:T(8,128)(2,1)}, bf16[8,256,512]{2,1,0:T(8,128)(2,1)}, u32[]{:S(2)}, u32[]{:S(2)}) collective-permute-start(bf16[8,256,512]{2,1,0:T(8,128)(2,1)} %get-tuple-element.128), channel_id=1, source_target_pairs={{0,1},{1,0},{2,3},{3,2},{4,5},{5,4},{6,7},{7,6},{8,9},{9,8},{10,11... | collective-permute-start | bytes 6291464 | tf_op jit(solution)/shard_map/ppermute | solution.py:839
  202.3 6.1 %copy-start.38 = (bf16[256,512]{1,0:T(8,128)(2,1)S(1)}, bf16[256,512]{1,0:T(8,128)(2,1)}, u32[]{:S(2)}) copy-start(bf16[256,512]{1,0:T(8,128)(2,1)} %get-tuple-element.110) | copy-start | bytes 786436
  204.4 28.8 %all-to-all-start.1 = ((bf16[4,2,128,512]{3,2,1,0:T(8,128)(2,1)}), bf16[4,2,128,512]{3,2,1,0:T(8,128)(2,1)S(1)}, u32[]{:S(2)}, u32[]{:S(2)}) async-start(bf16[4,2,128,512]{3,2,1,0:T(8,128)(2,1)} %maximum_bitcast_fusion), calls=%async_computation.1 | async-start | bytes 2097152 | tf_op jit(solution)/shard_map/all_to_all | solution.py:1000
  208.4 23.7 %collective-permute-start.4 = (bf16[256,512]{1,0:T(8,128)(2,1)S(1)}, bf16[256,512]{1,0:T(8,128)(2,1)S(1)}, u32[]{:S(2)}, u32[]{:S(2)}) collective-permute-start(bf16[256,512]{1,0:T(8,128)(2,1)S(1)} %copy-done.38), channel_id=1, source_target_pairs={{0,16},{16,0},{1,17},{17,1},{2,18},{18,2},{3,19},{19,3},{4,20},{20... | collective-permute-start | bytes 786440 | tf_op jit(solution)/shard_map/ppermute | solution.py:800
  232.0 6.9 %copy-start.16 = (bf16[256,512]{1,0:T(8,128)(2,1)}, bf16[256,512]{1,0:T(8,128)(2,1)S(1)}, u32[]{:S(2)}) copy-start(bf16[256,512]{1,0:T(8,128)(2,1)S(1)} %collective-permute-done.4.refs_21_) | copy-start | bytes 786436
  233.3 5.7 %copy-start.4 = (bf16[4,2,128,512]{3,2,1,0:T(8,128)(2,1)}, bf16[4,2,128,512]{3,2,1,0:T(8,128)(2,1)S(1)}, u32[]{:S(2)}) copy-start(bf16[4,2,128,512]{3,2,1,0:T(8,128)(2,1)S(1)} %all-to-all-done.1) | copy-start | bytes 3145732
  238.9 30.8 %all-to-all-start.2 = ((bf16[8,256,512]{2,1,0:T(8,128)(2,1)}), bf16[8,256,512]{2,1,0:T(8,128)(2,1)S(1)}, u32[]{:S(2)}, u32[]{:S(2)}) async-start(bf16[8,256,512]{2,1,0:T(8,128)(2,1)} %add_convert_fusion.1.refs_20_), calls=%async_computation.2 | async-start | bytes 4194304 | tf_op jit(solution)/shard_map/all_to_all | solution.py:874
  259.8 11.5 %collective-permute-start.6 = (bf16[8,192,512]{2,1,0:T(8,128)(2,1)}, bf16[8,192,512]{2,1,0:T(8,128)(2,1)}, u32[]{:S(2)}, u32[]{:S(2)}) collective-permute-start(bf16[8,192,512]{2,1,0:T(8,128)(2,1)} %get-tuple-element.130), channel_id=1, source_target_pairs={{0,1},{1,0},{2,3},{3,2},{4,5},{5,4},{6,7},{7,6},{8,9},{9,8},{10,11... | collective-permute-start | bytes 4718600 | tf_op jit(solution)/shard_map/ppermute | solution.py:839
  274.4 42.2 %all-to-all-start.3 = ((bf16[8,192,512]{2,1,0:T(8,128)(2,1)}), bf16[8,192,512]{2,1,0:T(8,128)(2,1)S(1)}, u32[]{:S(2)}, u32[]{:S(2)}) async-start(bf16[8,192,512]{2,1,0:T(8,128)(2,1)} %add_convert_fusion.3.refs_12_), calls=%async_computation.3 | async-start | bytes 3145728 | tf_op jit(solution)/shard_map/all_to_all | solution.py:874
  281.8 18.4 %copy-start.37 = (bf16[256,512]{1,0:T(8,128)(2,1)S(1)}, bf16[256,512]{1,0:T(8,128)(2,1)}, u32[]{:S(2)}) copy-start(bf16[256,512]{1,0:T(8,128)(2,1)} %get-tuple-element.145) | copy-start | bytes 786436
  300.1 17.9 %collective-permute-start.8 = (bf16[8,256,512]{2,1,0:T(8,128)(2,1)}, bf16[8,256,512]{2,1,0:T(8,128)(2,1)}, u32[]{:S(2)}, u32[]{:S(2)}) collective-permute-start(bf16[8,256,512]{2,1,0:T(8,128)(2,1)} %get-tuple-element.146), channel_id=1, source_target_pairs={{0,1},{1,0},{2,3},{3,2},{4,5},{5,4},{6,7},{7,6},{8,9},{9,8},{10,11... | collective-permute-start | bytes 6291464 | tf_op jit(solution)/shard_map/ppermute | solution.py:839
  300.2 15.2 %collective-permute-start.7 = (bf16[256,512]{1,0:T(8,128)(2,1)S(1)}, bf16[256,512]{1,0:T(8,128)(2,1)S(1)}, u32[]{:S(2)}, u32[]{:S(2)}) collective-permute-start(bf16[256,512]{1,0:T(8,128)(2,1)S(1)} %copy-done.37), channel_id=1, source_target_pairs={{0,16},{16,0},{1,17},{17,1},{2,18},{18,2},{3,19},{19,3},{4,20},{20... | collective-permute-start | bytes 786440 | tf_op jit(solution)/shard_map/ppermute | solution.py:800
  315.4 7.0 %copy-start.29 = (bf16[256,512]{1,0:T(8,128)(2,1)}, bf16[256,512]{1,0:T(8,128)(2,1)S(1)}, u32[]{:S(2)}) copy-start(bf16[256,512]{1,0:T(8,128)(2,1)S(1)} %collective-permute-done.7) | copy-start | bytes 786436
  322.4 30.5 %all-to-all-start.6 = ((bf16[8,256,512]{2,1,0:T(8,128)(2,1)}), bf16[8,256,512]{2,1,0:T(8,128)(2,1)S(1)}, u32[]{:S(2)}, u32[]{:S(2)}) async-start(bf16[8,256,512]{2,1,0:T(8,128)(2,1)} %add_convert_fusion.refs_23_), calls=%async_computation.6 | async-start | bytes 4194304 | tf_op jit(solution)/shard_map/all_to_all | solution.py:874
  342.8 3.9 collective-permute-start.10
  352.9 38.4 %all-to-all-start.4 = ((bf16[8,208,512]{2,1,0:T(8,128)(2,1)}), bf16[8,208,512]{2,1,0:T(8,128)(2,1)}, u32[]{:S(2)}, u32[]{:S(2)}) async-start(bf16[8,208,512]{2,1,0:T(8,128)(2,1)} %add_convert_fusion.2), calls=%async_computation.4 | async-start | bytes 3407872 | tf_op jit(solution)/shard_map/all_to_all | solution.py:874
  360.5 24.0 %copy-start.7 = (f32[128,512]{1,0:T(8,128)S(1)}, f32[128,512]{1,0:T(8,128)}, u32[]{:S(2)}) copy-start(f32[128,512]{1,0:T(8,128)} %param.22) | copy-start | bytes 786436
  360.5 24.0 %copy-start.25 = (f32[128,512]{1,0:T(8,128)S(1)}, f32[128,512]{1,0:T(8,128)}, u32[]{:S(2)}) copy-start(f32[128,512]{1,0:T(8,128)} %param.26) | copy-start | bytes 786436
  360.5 24.0 %copy-start.26 = (f32[128,512]{1,0:T(8,128)S(1)}, f32[128,512]{1,0:T(8,128)}, u32[]{:S(2)}) copy-start(f32[128,512]{1,0:T(8,128)} %param.30) | copy-start | bytes 786436
  360.5 23.8 %collective-permute-start.12 = (bf16[256,512]{1,0:T(8,128)(2,1)S(1)}, bf16[256,512]{1,0:T(8,128)(2,1)S(1)}, u32[]{:S(2)}, u32[]{:S(2)}) collective-permute-start(bf16[256,512]{1,0:T(8,128)(2,1)S(1)} %select_convert_fusion), channel_id=1, source_target_pairs={{0,16},{16,0},{1,17},{17,1},{2,18},{18,2},{3,19},{19,3},{4,20},{20... | collective-permute-start | bytes 786440 | tf_op jit(solution)/shard_map/ppermute | solution.py:800
  364.0 21.6 %copy-start.9 = (f32[32,2048]{1,0:T(8,128)S(1)}, f32[32,2048]{1,0:T(8,128)}, u32[]{:S(2)}) copy-start(f32[32,2048]{1,0:T(8,128)} %param.21) | copy-start | bytes 786436
  364.0 21.6 %copy-start.27 = (f32[32,2048]{1,0:T(8,128)S(1)}, f32[32,2048]{1,0:T(8,128)}, u32[]{:S(2)}) copy-start(f32[32,2048]{1,0:T(8,128)} %param.25) | copy-start | bytes 786436
  364.1 21.5 %copy-start.28 = (f32[32,2048]{1,0:T(8,128)S(1)}, f32[32,2048]{1,0:T(8,128)}, u32[]{:S(2)}) copy-start(f32[32,2048]{1,0:T(8,128)} %param.29) | copy-start | bytes 786436
  364.1 30.2 %collective-permute-start.9 = (bf16[256,512]{1,0:T(8,128)(2,1)}, bf16[256,512]{1,0:T(8,128)(2,1)}, u32[]{:S(2)}, u32[]{:S(2)}) collective-permute-start(bf16[256,512]{1,0:T(8,128)(2,1)} %get-tuple-element.148), channel_id=1, source_target_pairs={{0,16},{16,0},{1,17},{17,1},{2,18},{18,2},{3,19},{19,3},{4,20},{20... | collective-permute-start | bytes 786440 | tf_op jit(solution)/shard_map/ppermute | solution.py:800
  396.8 22.4 %all-to-all-start.5 = ((bf16[4,2,128,512]{3,2,1,0:T(8,128)(2,1)}), bf16[4,2,128,512]{3,2,1,0:T(8,128)(2,1)S(1)}, u32[]{:S(2)}, u32[]{:S(2)}) async-start(bf16[4,2,128,512]{3,2,1,0:T(8,128)(2,1)} %maximum_bitcast_fusion.1), calls=%async_computation.5 | async-start | bytes 2097152 | tf_op jit(solution)/shard_map/all_to_all | solution.py:1000
  401.0 15.5 %copy-start.23 = (f32[192,512]{1,0:T(8,128)S(1)}, f32[192,512]{1,0:T(8,128)}, u32[]{:S(2)}) copy-start(f32[192,512]{1,0:T(8,128)} %param.24) | copy-start | bytes 1179652
  401.0 15.5 %copy-start.24 = (f32[192,512]{1,0:T(8,128)S(1)}, f32[192,512]{1,0:T(8,128)}, u32[]{:S(2)}) copy-start(f32[192,512]{1,0:T(8,128)} %param.28) | copy-start | bytes 1179652
  401.0 15.3 %collective-permute-start.11 = (bf16[208,512]{1,0:T(8,128)(2,1)S(1)}, bf16[208,512]{1,0:T(8,128)(2,1)S(1)}, u32[]{:S(2)}, u32[]{:S(2)}) collective-permute-start(bf16[208,512]{1,0:T(8,128)(2,1)S(1)} %select_convert_fusion.1), channel_id=1, source_target_pairs={{0,16},{16,0},{1,17},{17,1},{2,18},{18,2},{3,19},{19,3},{4,20},{20... | collective-permute-start | bytes 638984 | tf_op jit(solution)/shard_map/ppermute | solution.py:800
  401.8 15.9 %copy-start.32 = (f32[160]{0:T(256)S(1)}, f32[160]{0:T(256)}, u32[]{:S(2)}) copy-start(f32[160]{0:T(256)} %param.23) | copy-start | bytes 1924
  401.8 15.9 %copy-start.35 = (f32[160]{0:T(256)S(1)}, f32[160]{0:T(256)}, u32[]{:S(2)}) copy-start(f32[160]{0:T(256)} %param.27) | copy-start | bytes 1924
  401.9 15.9 %copy-start.36 = (f32[160]{0:T(256)S(1)}, f32[160]{0:T(256)}, u32[]{:S(2)}) copy-start(f32[160]{0:T(256)} %param.31) | copy-start | bytes 1924
  417.6 20.6 %copy-start.13 = (f32[192,512]{1,0:T(8,128)}, f32[192,512]{1,0:T(8,128)S(1)}, u32[]{:S(2)}) copy-start(f32[192,512]{1,0:T(8,128)S(1)} %get-tuple-element.174) | copy-start | bytes 1179652
  417.6 20.6 %copy-start.14 = (f32[192,512]{1,0:T(8,128)}, f32[192,512]{1,0:T(8,128)S(1)}, u32[]{:S(2)}) copy-start(f32[192,512]{1,0:T(8,128)S(1)} %get-tuple-element.175) | copy-start | bytes 1179652
  417.6 17.7 %copy-start.19 = (f32[128,512]{1,0:T(8,128)S(1)}, f32[128,512]{1,0:T(8,128)}, u32[]{:S(2)}) copy-start(f32[128,512]{1,0:T(8,128)} %get-tuple-element.179) | copy-start | bytes 786436
  417.6 17.7 %copy-start.20 = (f32[128,512]{1,0:T(8,128)S(1)}, f32[128,512]{1,0:T(8,128)}, u32[]{:S(2)}) copy-start(f32[128,512]{1,0:T(8,128)} %get-tuple-element.180) | copy-start | bytes 786436
  421.1 12.5 %all-to-all-start.7 = ((f32[32,8,128]{2,1,0:T(8,128)}), f32[32,8,128]{2,1,0:T(8,128)S(1)}, u32[]{:S(2)}, u32[]{:S(2)}) async-start(f32[32,8,128]{2,1,0:T(8,128)} %broadcast_in_dim.170), calls=%async_computation.7 | async-start | bytes 262144 | tf_op jit(solution)/shard_map/all_to_all | solution.py:1061
  (14 other events, 54.4 us)
Sparse Core Ops, SparseCore 0:
  49.3 71.0 all-gather.4
  122.6 41.3 all-gather.6
